TPU v7x, 256 devices: a whole 4x4x8 slice. The times are simulated.
256 devices in a mesh: region: 8 (over y, z_lo), slab: 32 (over z_hi, x, core).
Axes of the slice: x: 4, y: 4, z: 8 (z_hi: 4, z_lo: 2; z = z_hi * 2 + z_lo), core: 2. Of those that a mesh axis runs over, the one named last changes fastest.
Arguments:
- magnetic: float32 [3, 512, 64, 1024], P(None, 'slab', None, 'region'), may hold values from -6 to 6
- velocity: float32 [3, 512, 64, 1024], P(None, 'slab', None, 'region'), may hold values from -12 to 12
- wall_response: float32 [1024, 512, 512], P(('region', 'slab')), may hold values from -0.25 to 0.25
- mode_slots: int32 [1024], replicated, may hold values from 0 to 1023, each once
- wall_layers: int32 [1024], P('region'), may hold values from 1 to 8
Outputs:
- magnetic_next: float32 [3, 512, 64, 1024], P(None, 'slab', None, 'region')
- wall_flux: float32 [2, 512, 1024], P(None, 'slab', 'region')
Inputs may be any that keep to these rules, and one draw needn't show every extreme that they name: `mode_slots`: each slot names a different mode.
All inputs are finite; a program needn't handle non-finite values.
Results may differ from a plain program's by a relative error of at most 0.00007.
Values sent between devices are 32-bit elements; how exact they have to be, the bound alone decides.
No kernel may reach another device: no remote copies, remote signals or barrier semaphores. Data moves between devices by JAX's collectives and lax.ppermute only.
A program may use at most 128 MiB of HBM per device.

v0:
```python
import math

import jax
import jax.numpy as jnp
from jax import lax
from jax.sharding import PartitionSpec as P

LW = 8


TIME_STEP = 0.0003
DIFFUSIVITY = 0.001
RADIAL_STEP = 1.0 / 384.0
AXIAL_STEP = 1.0 / 768.0
HIGHEST = lax.Precision.HIGHEST


def with_halo(block, sides, width, periodic):
    for axis, dim in sides:
        count = lax.axis_size(axis)
        forward = [(i, i + 1) for i in range(count - 1)]
        if periodic:
            forward.append((count - 1, 0))
        backward = [(target, source) for source, target in forward]
        low = lax.ppermute(
            lax.slice_in_dim(block, block.shape[dim] - width, None, axis=dim), axis, forward
        )
        high = lax.ppermute(lax.slice_in_dim(block, 0, width, axis=dim), axis, backward)
        block = jnp.concatenate([low, block, high], axis=dim)
    return block


def basis_table(modes, cells, azimuth_total):
    frequency = (modes + 1) // 2
    phase = frequency[:, None] * (2 * cells[None, :] + 1) % (2 * azimuth_total)
    angle = phase.astype(jnp.float32) * (math.pi / azimuth_total)
    return jnp.where((modes % 2 == 1)[:, None], jnp.sin(angle), jnp.cos(angle))


def mode_weight(modes, azimuth_total):
    single = (modes == 0) | (modes == azimuth_total - 1)
    return jnp.where(single, 1.0, 2.0).astype(jnp.float32) / azimuth_total


def radius_column(radial_cells):
    index = jnp.arange(radial_cells).astype(jnp.float32)
    return (1.0 - (radial_cells - index - 0.5) * RADIAL_STEP)[:, None]


def advance(
    center_b,
    center_u,
    radial_b,
    radial_u,
    azimuth_b,
    azimuth_u,
    axial_b,
    axial_u,
    radius,
    angle_step,
):
    inv_radial = 1.0 / (2.0 * RADIAL_STEP)
    inv_azimuth = 1.0 / (2.0 * radius * angle_step)
    inv_axial = 1.0 / (2.0 * AXIAL_STEP)
    grad_b = (
        (radial_b[0] - radial_b[1]) * inv_radial,
        (azimuth_b[0] - azimuth_b[1]) * inv_azimuth,
        (axial_b[0] - axial_b[1]) * inv_axial,
    )
    grad_u = (
        (radial_u[0] - radial_u[1]) * inv_radial,
        (azimuth_u[0] - azimuth_u[1]) * inv_azimuth,
        (axial_u[0] - axial_u[1]) * inv_axial,
    )
    laplace = (radial_b[0] - 2.0 * center_b + radial_b[1]) / RADIAL_STEP**2
    laplace = laplace + grad_b[0] / radius
    laplace = laplace + (azimuth_b[0] - 2.0 * center_b + azimuth_b[1]) / (radius * angle_step) ** 2
    laplace = laplace + (axial_b[0] - 2.0 * center_b + axial_b[1]) / AXIAL_STEP**2
    carried = center_u[0] * grad_b[0] + center_u[1] * grad_b[1] + center_u[2] * grad_b[2]
    stretched = center_b[0] * grad_u[0] + center_b[1] * grad_u[1] + center_b[2] * grad_u[2]
    return center_b + TIME_STEP * (DIFFUSIVITY * laplace - carried + stretched)


def shards(magnetic, velocity, wall_response, mode_slots, wall_layers):
    axial_cells = magnetic.shape[1]
    radial_cells = magnetic.shape[2]
    azimuth_cells = magnetic.shape[3]
    azimuth_total = mode_slots.shape[0]
    mode_count = wall_response.shape[0]
    region_index = lax.axis_index("region")
    slab_index = lax.axis_index("slab")
    trace = magnetic[1:3, :, radial_cells - 1, :]
    trace_flat = trace.reshape(2 * axial_cells, azimuth_cells)
    local_cells = region_index * azimuth_cells + jnp.arange(azimuth_cells, dtype=jnp.int32)
    own_modes = lax.dynamic_slice_in_dim(mode_slots, region_index * azimuth_cells, azimuth_cells)
    table = basis_table(mode_slots, local_cells, azimuth_total)
    coefficients = lax.psum_scatter(
        jnp.dot(table, trace_flat.T, precision=HIGHEST), "region", scatter_dimension=0, tiled=True
    )
    by_mode = coefficients.reshape(azimuth_cells, 2, axial_cells)
    all_axial = lax.all_gather(by_mode, "slab", axis=2, tiled=True)
    mine = lax.dynamic_slice_in_dim(all_axial, slab_index * mode_count, mode_count, 0)
    applied = jnp.einsum("szy,scy->scz", wall_response, mine, precision=HIGHEST)
    all_slots = lax.all_gather(applied, "slab", axis=0, tiled=True)
    returned = lax.dynamic_slice_in_dim(all_slots, slab_index * axial_cells, axial_cells, 2)
    returned_flat = returned.reshape(azimuth_cells, 2 * axial_cells)
    scaled = returned_flat * mode_weight(own_modes, azimuth_total)[:, None]
    cells = jnp.arange(azimuth_cells * lax.axis_size("region"), dtype=jnp.int32)
    table = basis_table(own_modes, cells, azimuth_total)
    flux_rows = lax.psum_scatter(
        jnp.dot(table.T, scaled, precision=HIGHEST), "region", scatter_dimension=0, tiled=True
    )
    wall_flux = flux_rows.reshape(azimuth_cells, 2, axial_cells).transpose(1, 2, 0)
    thickness = wall_layers.astype(jnp.float32) / LW
    ghost = jnp.concatenate(
        [magnetic[0:1, :, radial_cells - 1, :], trace - thickness * wall_flux], 0
    )
    both = jnp.concatenate([magnetic, velocity], 0)
    axial_ext = with_halo(both, (("slab", 1),), 1, False)
    azimuth_ext = with_halo(both, (("region", 3),), 1, True)
    outer_edge = jnp.concatenate([ghost, velocity[:, :, radial_cells - 1, :]], 0)
    radial_ext = jnp.concatenate([both[:, :, :1], both, outer_edge[:, :, None]], 2)
    radial_b = (radial_ext[:3, :, 2:], radial_ext[:3, :, :-2])
    radial_u = (radial_ext[3:, :, 2:], radial_ext[3:, :, :-2])
    azimuth_b = (azimuth_ext[:3, ..., 2:], azimuth_ext[:3, ..., :-2])
    azimuth_u = (azimuth_ext[3:, ..., 2:], azimuth_ext[3:, ..., :-2])
    axial_b = (axial_ext[:3, 2:], axial_ext[:3, :-2])
    axial_u = (axial_ext[3:, 2:], axial_ext[3:, :-2])
    radius = radius_column(radial_cells)
    angle_step = 2.0 * math.pi / azimuth_total
    magnetic_next = advance(
        magnetic,
        velocity,
        radial_b,
        radial_u,
        azimuth_b,
        azimuth_u,
        axial_b,
        axial_u,
        radius,
        angle_step,
    )
    return (magnetic_next, wall_flux)


def solution(mesh):
    placed = (
        P(None, "slab", None, "region"),
        P(None, "slab", None, "region"),
        P(("region", "slab"), None, None),
        P(),
        P("region"),
    )
    return jax.shard_map(
        shards,
        mesh=mesh,
        in_specs=placed,
        out_specs=(P(None, "slab", None, "region"), P(None, "slab", "region")),
        check_vma=False,
    )
```

profile of v0, /device:TPU:2, one launch (start us, length us, event | category | flops | bytes accessed | tf_op | source)
XLA Modules:
  0.0 230.6 jit_solution(1849004988606257779)
XLA Ops:
  7.2 0.7 add_select_fusion.2
  7.9 0.7 fusion.55
  8.6 0.9 slice.91
  9.5 4.4 %fusion.21 = f32[1024,32]{0,1:T(8,128)} fusion(f32[32,128]{1,0:T(8,128)S(1)} %bitcast.36, s32[128]{0:T(128)S(1)} %multiply_add_fusion.1, s32[1024]{0:T(1024)S(1)} %add_select_fusion.2, pred[1024]{0:T(1024)(128)(4,1)S(1)} %fusion.55), kind=kOutput, calls=%fused_computation.61 | convolution fusion | flops 52297728 | bytes 153088 | tf_op jit(solution)/shard_map/dot_general | solution.py:98
  14.0 2.3 copy.99
  16.3 3.3 %copy.80 = f32[3,16,64,128]{2,1,3,0:T(8,128)} copy(f32[3,16,64,128]{3,2,1,0:T(8,128)} %param.6) | data formatting | bytes 3145728 | tf_op args[1]
  19.6 3.3 %fusion.37 = (f32[6,1,64,128]{2,1,3,0:T(1,128)}, f32[6,1,64,128]{2,1,3,0:T(1,128)S(1)}) fusion(f32[3,16,64,128]{2,1,3,0:T(8,128)S(1)} %copy.99, f32[3,16,64,128]{2,1,3,0:T(8,128)} %copy.80), kind=kLoop, calls=%fused_computation.75 | loop fusion | flops 98304 | bytes 3538944 | tf_op jit(solution)/shard_map/concatenate | solution.py:118
  23.0 1.8 copy.89
  24.8 1.9 collective-permute-start.2
  26.7 0.9 copy.91
  27.6 2.4 %collective-permute-start.3 = (f32[6,1,64,128]{3,2,1,0:T(8,128)}, f32[6,1,64,128]{3,2,1,0:T(8,128)}, u32[]{:S(2)}, u32[]{:S(2)}) collective-permute-start(f32[6,1,64,128]{3,2,1,0:T(8,128)} %copy.91), channel_id=1, source_target_pairs={{0,1},{1,2},{2,3},{3,4},{4,5},{5,6},{6,7},{7,8},{8,9},{9,10},{10,1... | collective-permute-start | bytes 589832 | tf_op jit(solution)/shard_map/ppermute | solution.py:25
  30.0 1.4 fusion.52
  31.4 4.4 %collective-permute-start = (f32[6,16,64,1]{2,1,3,0:T(8,128)}, f32[6,16,64,1]{2,1,3,0:T(8,128)}, u32[]{:S(2)}, u32[]{:S(2)}) collective-permute-start(f32[6,16,64,1]{2,1,3,0:T(8,128)} %get-tuple-element.12), channel_id=1, source_target_pairs={{32,0},{64,32},{96,64},{128,96},{160,128},{192,160},{224,192},{0,2... | collective-permute-start | bytes 73736 | tf_op jit(solution)/shard_map/ppermute | solution.py:28
  35.8 0.9 fusion.59
  36.7 0.8 and_select_fusion
  37.5 0.8 fusion.58
  38.2 2.6 %multiply_bitcast_fusion.3 = (f32[16,64,128]{2,1,0:T(8,128)}, f32[16,64,128]{2,1,0:T(8,128)}, f32[16,64,128]{2,1,0:T(8,128)}) fusion(f32[3,16,64,128]{3,2,1,0:T(8,128)} %param.6), kind=kLoop, calls=%fused_computation.60 | loop fusion | flops 262144 | bytes 3145728 | tf_op jit(solution)/shard_map/mul | solution.py:79
  40.9 1.2 multiply_bitcast_fusion.1
  42.1 0.6 multiply_divide_fusion
  42.7 5.3 %fusion = f32[6,16,1,128]{2,1,3,0:T(8,128)} fusion(f32[3,16,64,128]{2,1,3,0:T(8,128)S(1)} %copy.99, f32[3,16,64,128]{2,1,3,0:T(8,128)} %copy.80), kind=kLoop, calls=%fused_computation.8 | loop fusion | flops 12288 | bytes 3194880 | tf_op jit(solution)/shard_map/concatenate | solution.py:118
  48.0 8.7 %reduce-scatter.3.cloned.1.call-done = f32[128,32]{0,1:T(8,128)} async-done(((f32[1024,32]{0,1:T(8,128)}), f32[128,32]{0,1:T(8,128)}) %reduce-scatter.3.cloned.1.call-update) | async-done | bytes 16400 | tf_op jit(solution)/shard_map/reduce_scatter | solution.py:97
  56.7 0.7 copy.83
  57.5 40.9 %all_gather.6 = f32[128,2,512]{0,1,2:T(2,128)S(1)} all-gather(f32[128,2,16]{0,1,2:T(2,128)S(1)} %copy.83), channel_id=1, replica_groups=mesh['region'=8,'slab'=32] {'slab'}, dimensions={2}, use_global_device_ids=true | all-gather | bytes 540672 | tf_op jit(solution)/shard_map/all_gather | solution.py:101
  98.3 1.4 constant_dynamic-slice_fusion.1
  99.7 1.2 copy.103
  100.9 5.7 %fusion.69 = f32[4,2,512]{2,1,0:T(2,128)S(1)} fusion(f32[4,2,512]{2,1,0:T(2,128)S(1)} %copy.103, f32[4,512,512]{2,1,0:T(8,128)} %param.7), kind=kOutput, calls=%fused_computation.135 | convolution fusion | flops 25165824 | bytes 4227072 | tf_op jit(solution)/shard_map/szy,scy->scz/dot_general | solution.py:103
  106.6 45.8 %all_gather.7 = f32[128,2,512]{2,1,0:T(2,128)S(1)} all-gather(f32[4,2,512]{2,1,0:T(2,128)S(1)} %fusion.69), channel_id=1, replica_groups=mesh['region'=8,'slab'=32] {'slab'}, dimensions={0}, use_global_device_ids=true | all-gather | bytes 540672 | tf_op jit(solution)/shard_map/all_gather | solution.py:104
  152.4 0.2 constant_dynamic-slice_fusion
  152.7 3.2 %fusion.26 = f32[1024,32]{0,1:T(8,128)} fusion(f32[128,32]{0,1:T(8,128)S(1)} %bitcast_multiply_fusion, s32[1024]{0:T(1024)S(1)} %multiply_add_fusion, s32[128]{0:T(128)S(1)} %and_select_fusion, pred[128]{0:T(512)(128)(4,1)S(1)} %fusion.58), kind=kOutput, calls=%fused_computation.65 | convolution fusion | flops 52297728 | bytes 152192 | tf_op jit(solution)/shard_map/dot_general | solution.py:111
  156.0 0.5 multiply_subtract_fusion.2
  156.5 1.6 slice.92
  158.1 1.4 slice.90
  159.5 2.4 %copy.93 = f32[16,64,128]{1,0,2:T(8,128)} copy(f32[16,64,128]{2,1,0:T(8,128)} %get-tuple-element.16) | data formatting | bytes 1048576 | tf_op jit(solution)/shard_map/mul | solution.py:79
  162.0 2.4 %copy.94 = f32[16,64,128]{1,0,2:T(8,128)} copy(f32[16,64,128]{2,1,0:T(8,128)} %get-tuple-element.18) | data formatting | bytes 1048576 | tf_op jit(solution)/shard_map/mul | solution.py:79
  164.4 2.5 %copy.95 = f32[16,64,128]{1,0,2:T(8,128)} copy(f32[16,64,128]{2,1,0:T(8,128)} %get-tuple-element.17) | data formatting | bytes 1048576 | tf_op jit(solution)/shard_map/mul | solution.py:79
  166.9 2.5 %copy.96 = f32[16,64,128]{1,0,2:T(8,128)} copy(f32[16,64,128]{2,1,0:T(8,128)} %get-tuple-element.19) | data formatting | bytes 1048576 | tf_op jit(solution)/shard_map/mul | solution.py:80
  169.4 2.4 %copy.97 = f32[16,64,128]{1,0,2:T(8,128)} copy(f32[16,64,128]{2,1,0:T(8,128)} %get-tuple-element.20) | data formatting | bytes 1048576 | tf_op jit(solution)/shard_map/mul | solution.py:80
  171.8 2.4 %copy.98 = f32[16,64,128]{1,0,2:T(8,128)} copy(f32[16,64,128]{2,1,0:T(8,128)} %get-tuple-element.21) | data formatting | bytes 1048576 | tf_op jit(solution)/shard_map/mul | solution.py:80
  174.2 0.6 convert_multiply_fusion
  174.8 1.2 copy.90
  176.0 1.8 copy.92
  177.8 12.7 %reduce-scatter.5.cloned.1.call-done = f32[128,32]{0,1:T(8,128)} async-done(((f32[1024,32]{0,1:T(8,128)}), f32[128,32]{0,1:T(8,128)}) %reduce-scatter.5.cloned.1.call-update) | async-done | bytes 16400 | tf_op jit(solution)/shard_map/reduce_scatter | solution.py:110
  190.6 0.7 multiply_subtract_fusion.1
  191.3 1.4 maximum_bitcast_fusion
  192.6 4.9 %copy.87 = f32[6,16,1,128]{2,1,3,0:T(8,128)} copy(f32[6,16,1,128]{3,1,0,2:T(8,128)} %maximum_bitcast_fusion) | data formatting | bytes 98304 | tf_op jit(solution)/shard_map/broadcast_in_dim | solution.py:122
  197.6 10.2 %pad_maximum_fusion = (f32[6,16,65,128]{2,1,3,0:T(8,128)S(1)}, f32[6,16,65,128]{2,1,3,0:T(8,128)}) fusion(f32[6,16,1,128]{2,1,3,0:T(8,128)} %copy.87, f32[3,16,64,128]{2,1,3,0:T(8,128)} %copy.80, f32[3,16,64,128]{2,1,3,0:T(8,128)S(1)} %copy.99, f32[6,16,1,128]{2,1,3,0:T(8,128)} %fusion), kind=kLoop, calls=%fused_computation.9 | loop fusion | flops 3194880 | bytes 9633792 | tf_op jit(solution)/shard_map/concatenate | solution.py:122
  207.8 12.7 %fusion.6 = f32[3,16,64,128]{2,1,3,0:T(8,128)} fusion(f32[3,16,64,128]{2,1,3,0:T(8,128)S(1)} %copy.99, f32[6,1,64,128]{2,1,3,0:T(1,128)} %copy.92, f32[3,16,64,128]{2,1,3,0:T(8,128)S(1)} %copy-done, f32[6,1,64,128]{2,1,3,0:T(1,128)S(1)} %copy.90, f32[6,16,64,1]{2,1,3,0:T(8,128)} %collective-permute-done.1, f32[6,16,64,1]{2,1,3,0:T(8,128)} %collective-permute-done, ...), kind=kLoop, calls=%fused_computation.17 | loop fusion | flops 21233664 | bytes 14598912 | tf_op jit(solution)/shard_map/add | solution.py:81
  220.5 3.2 %copy.100 = f32[3,16,64,128]{3,2,1,0:T(8,128)} copy(f32[3,16,64,128]{2,1,3,0:T(8,128)} %fusion.6) | data formatting | bytes 3145728
  (25 shorter events, 0.2 us)
Async XLA Ops:
  7.2 49.6 %reduce-scatter.3.cloned.1.call-start = ((), (), s32[]{:S(2)}) async-start(), calls=%async_computation.2 | async-start | bytes 147456 | tf_op jit(solution)/shard_map/reduce_scatter | solution.py:97
  14.0 176.6 %reduce-scatter.5.cloned.1.call-start = ((), (), s32[]{:S(2)}) async-start(), calls=%async_computation.3 | async-start | bytes 147456 | tf_op jit(solution)/shard_map/reduce_scatter | solution.py:110
  24.8 150.0 %collective-permute-start.2 = (f32[6,1,64,128]{3,2,1,0:T(8,128)}, f32[6,1,64,128]{3,2,1,0:T(8,128)}, u32[]{:S(2)}, u32[]{:S(2)}) collective-permute-start(f32[6,1,64,128]{3,2,1,0:T(8,128)} %copy.89), channel_id=1, source_target_pairs={{1,0},{2,1},{3,2},{4,3},{5,4},{6,5},{7,6},{8,7},{9,8},{10,9},{11,1... | collective-permute-start | bytes 589832 | tf_op jit(solution)/shard_map/ppermute | solution.py:28
  27.6 148.4 %collective-permute-start.3 = (f32[6,1,64,128]{3,2,1,0:T(8,128)}, f32[6,1,64,128]{3,2,1,0:T(8,128)}, u32[]{:S(2)}, u32[]{:S(2)}) collective-permute-start(f32[6,1,64,128]{3,2,1,0:T(8,128)} %copy.91), channel_id=1, source_target_pairs={{0,1},{1,2},{2,3},{3,4},{4,5},{5,6},{6,7},{7,8},{8,9},{9,10},{10,1... | collective-permute-start | bytes 589832 | tf_op jit(solution)/shard_map/ppermute | solution.py:25
  31.4 176.3 %collective-permute-start = (f32[6,16,64,1]{2,1,3,0:T(8,128)}, f32[6,16,64,1]{2,1,3,0:T(8,128)}, u32[]{:S(2)}, u32[]{:S(2)}) collective-permute-start(f32[6,16,64,1]{2,1,3,0:T(8,128)} %get-tuple-element.12), channel_id=1, source_target_pairs={{32,0},{64,32},{96,64},{128,96},{160,128},{192,160},{224,192},{0,2... | collective-permute-start | bytes 73736 | tf_op jit(solution)/shard_map/ppermute | solution.py:28
  35.8 171.9 %collective-permute-start.1 = (f32[6,16,64,1]{2,1,3,0:T(8,128)}, f32[6,16,64,1]{2,1,3,0:T(8,128)}, u32[]{:S(2)}, u32[]{:S(2)}) collective-permute-start(f32[6,16,64,1]{2,1,3,0:T(8,128)} %get-tuple-element.13), channel_id=1, source_target_pairs={{0,32},{32,64},{64,96},{96,128},{128,160},{160,192},{192,224},{224... | collective-permute-start | bytes 73736 | tf_op jit(solution)/shard_map/ppermute | solution.py:25
  35.8 5.1 %copy-start.1 = (f32[3,16,64,128]{3,2,1,0:T(8,128)S(1)}, f32[3,16,64,128]{3,2,1,0:T(8,128)}, u32[]{:S(2)}) copy-start(f32[3,16,64,128]{3,2,1,0:T(8,128)} %param.5) | copy-start | bytes 4718596
  164.4 9.8 %copy-start.5 = (s32[128]{0:T(128)S(1)}, s32[128]{0:T(128)}, u32[]{:S(2)}) copy-start(s32[128]{0:T(128)} %param.9) | copy-start | bytes 1540
  197.5 10.2 %copy-start = (f32[3,16,64,128]{2,1,3,0:T(8,128)S(1)}, f32[3,16,64,128]{2,1,3,0:T(8,128)}, u32[]{:S(2)}) copy-start(f32[3,16,64,128]{2,1,3,0:T(8,128)} %copy.80) | copy-start | bytes 4718596
  197.5 10.2 %copy-start.2 = (f32[64]{0:T(128)S(1)}, f32[64]{0:T(128)}, u32[]{:S(2)}) copy-start(f32[64]{0:T(128)} %get-tuple-element.22) | copy-start | bytes 772
  197.5 10.2 %copy-start.3 = (f32[64]{0:T(128)S(1)}, f32[64]{0:T(128)}, u32[]{:S(2)}) copy-start(f32[64]{0:T(128)} %get-tuple-element.23) | copy-start | bytes 772
  197.5 10.2 %copy-start.4 = (f32[64]{0:T(128)S(1)}, f32[64]{0:T(128)}, u32[]{:S(2)}) copy-start(f32[64]{0:T(128)} %multiply_subtract_fusion.2) | copy-start | bytes 772
Sparse Core Ops, SparseCore 0:
  14.1 42.5 reduce-scatter.2
  156.1 34.4 reduce-scatter.4
where the time goes:
time: 232 us; the launch traced here: 231 us
  blocking collectives  86.7 us (37%)
  other arithmetic  44.5 us (19%)
  local copies, waits for them, and re-layouts  41.7 us (18%)
  waiting for transfers between devices  21.5 us (9%)
  between operations  14.2 us (6%)
  matrix products  13.3 us (6%)
  starting transfers between devices  8.76 us (4%)
    all_gather x1, blocking collectives, shards(): all_slots = lax.all_gather(applied, 'slab', axis=0, tiled=True)  45.8 us
    all_gather x1, blocking collectives, shards(): all_axial = lax.all_gather(by_mode, 'slab', axis=2, tiled=True)  40.9 us
    add x1, other arithmetic, advance(): return center_b + TIME_STEP * (DIFFUSIVITY * laplace - carried + stretched)  12.7 us
    reduce_scatter x1, waiting for transfers between devices, shards(): lax.psum_scatter(jnp.dot(table.T, scaled, precision=HIGHEST), 'region', s...  12.7 us
    concatenate x1, other arithmetic, shards(): jnp.concatenate([both[:, :, :1], both, outer_edge[:, :, None]], 2)  10.2 us
    unnamed x17, local copies, waits for them, and re-layouts  10.1 us
    concatenate x3, other arithmetic, shards(): both = jnp.concatenate([magnetic, velocity], 0)  10.1 us
    reduce_scatter x1, waiting for transfers between devices, shards(): lax.psum_scatter(jnp.dot(table, trace_flat.T, precision=HIGHEST), 'region...  8.74 us
  transfers between devices with their start and end apart: 6, of which 2 were waited for; matrix products, arithmetic and copies ran while one was open for 33% of the time, Pallas kernels for 0%

commit v1 on v0

v1 whole, which is shorter than its diff:
```python
import math

import jax
import jax.numpy as jnp
from jax import lax
from jax.experimental import pallas as pl
from jax.experimental.pallas import tpu as pltpu
from jax.sharding import PartitionSpec as P

LW = 8
TIME_STEP = 0.0003
DIFFUSIVITY = 0.001
RADIAL_STEP = 1.0 / 384.0
AXIAL_STEP = 1.0 / 768.0

F32 = jnp.float32
BF16 = jnp.bfloat16
BOTH = ("region", "slab")
VMEM = pl.BlockSpec(memory_space=pltpu.VMEM)
ANY = pl.BlockSpec(memory_space=pl.ANY)
NT = (((1,), (1,)), ((), ()))
NN = (((1,), (0,)), ((), ()))


def params(mib):
    return pltpu.CompilerParams(vmem_limit_bytes=mib * 1024 * 1024)


def cost(flops, nbytes):
    return pl.CostEstimate(flops=flops, bytes_accessed=nbytes, transcendentals=0)


def lanes(shape):
    return lax.broadcasted_iota(jnp.int32, shape, len(shape) - 1)


def rows(shape):
    return lax.broadcasted_iota(jnp.int32, shape, len(shape) - 2)


def split(x):
    high = x.astype(BF16)
    return high, (x - high.astype(F32)).astype(BF16)


def dot(a, b, dims):
    return lax.dot_general(a, b, dims, preferred_element_type=F32)


def dot3(a, b, dims):
    ah, al = a
    bh, bl = b
    return dot(ah, bh, dims) + (dot(ah, bl, dims) + dot(al, bh, dims))


def half_turn_sine(phase, total):
    half = phase - total
    fold = jnp.abs(half)
    fold = jnp.minimum(fold, total - fold)
    x = fold.astype(F32) * (math.pi / total)
    y = x * x
    poly = -1.0 / math.factorial(11)
    for n, sign in ((9, 1.0), (7, -1.0), (5, 1.0), (3, -1.0)):
        poly = poly * y + sign / math.factorial(n)
    value = x + x * (y * poly)
    return jnp.where(half < 0, value, -value)


def block_transpose(x, width):
    r, b = rows(x.shape), lanes(x.shape) // width
    n, m = x.shape
    for bit in range(3):
        h = 1 << bit
        down = pltpu.roll(pltpu.roll(x, h, 0), m - width * h, 1)
        up = pltpu.roll(pltpu.roll(x, n - h, 0), width * h, 1)
        rb, bb = (r >> bit) & 1, (b >> bit) & 1
        x = jnp.where(rb == bb, x, jnp.where(rb == 1, down, up))
    return x


def encode_kernel(mag, modes, message, table, edge, coeff, sem):
    nmodes, cells = table.shape
    copy = pltpu.make_async_copy(mag.at[1:3, :, 56:64, :], edge, sem)
    copy.start()
    first = lax.axis_index("region") * cells
    odd_cell = (2 * (first + lanes((cells, cells))) + 1).astype(F32)
    columns = jnp.transpose(modes[...].astype(F32), (1, 0))
    for j in range(nmodes // cells):
        mode = jnp.broadcast_to(columns[:, j : j + 1], (cells, cells)).astype(jnp.int32)
        phase = (((mode + 1) >> 1).astype(F32) * odd_cell).astype(jnp.int32)
        phase = jnp.where((mode & 1) == 1, phase, phase + nmodes // 2) & (2 * nmodes - 1)
        table[j * cells : (j + 1) * cells, :] = half_turn_sine(phase, nmodes)
    copy.wait()
    trace = edge[:, :, 7, :].reshape(32, cells)
    trace = split(jnp.concatenate([trace] * 4, 0))
    coeff[...] = dot3(split(table[...]), trace, NT)
    count = nmodes // 4
    lane = lanes((count, 128)) // 32
    out = coeff[pl.ds(0, count, stride=4), :]
    for i in range(1, 4):
        out = jnp.where(lane == i, coeff[pl.ds(i, count, stride=4), :], out)
    message[...] = out


def encode(mag, modes):
    cells = mag.shape[3]
    nmodes = modes.size
    return pl.pallas_call(
        encode_kernel,
        out_shape=(
            jax.ShapeDtypeStruct((nmodes // 4, 128), F32),
            jax.ShapeDtypeStruct((nmodes, cells), F32),
        ),
        in_specs=[ANY, VMEM],
        out_specs=(VMEM, VMEM),
        scratch_shapes=[
            pltpu.VMEM((2, 16, 8, cells), F32),
            pltpu.VMEM((nmodes, 128), F32),
            pltpu.SemaphoreType.DMA,
        ],
        compiler_params=params(8),
        cost_estimate=cost(3 * 2 * 1024 * 128 * 128, 1 << 20),
        name="encode",
    )(mag, modes.reshape(8, 128))


def weigh_kernel(table, modes, high, low, scaled):
    nmodes, cells = table.shape
    columns = jnp.transpose(modes[...].astype(F32), (1, 0))
    for j in range(nmodes // cells):
        mode = jnp.broadcast_to(columns[:, j : j + 1], (cells, cells))
        single = (mode == 0.0) | (mode == float(nmodes - 1))
        part = slice(j * cells, (j + 1) * cells)
        scaled[part, :] = table[part, :] * jnp.where(single, 1.0 / nmodes, 2.0 / nmodes)
    for i in range(4):
        high[i], low[i] = split(scaled[pl.ds(i, nmodes // 4, stride=4), :])


def weigh(table, modes):
    nmodes, cells = table.shape
    shape = jax.ShapeDtypeStruct((4, nmodes // 4, cells), BF16)
    return pl.pallas_call(
        weigh_kernel,
        out_shape=(shape, shape),
        in_specs=[VMEM, VMEM],
        out_specs=(VMEM, VMEM),
        scratch_shapes=[pltpu.VMEM((nmodes, cells), F32)],
        compiler_params=params(8),
        cost_estimate=cost(1 << 20, 1 << 20),
        name="weigh",
    )(table, modes.reshape(8, 128))


def halves_kernel(wall, high, low):
    high[...], low[...] = split(wall[...])


def halves(wall):
    shape = jax.ShapeDtypeStruct(wall.shape, BF16)
    block = pl.BlockSpec((1, *wall.shape[1:]), lambda i: (i, 0, 0))
    return pl.pallas_call(
        halves_kernel,
        out_shape=(shape, shape),
        grid=(wall.shape[0],),
        in_specs=[block],
        out_specs=(block, block),
        compiler_params=params(12),
        cost_estimate=cost(4 << 20, 8 << 20),
        name="halves",
    )(wall)


def wall_kernel(arrived, high, low, message):
    x = arrived[0:32, :]
    for r in range(1, 8):
        x = x + arrived[r * 32 : (r + 1) * 32, :]
    x = block_transpose(x, 16)
    coeff = jnp.concatenate([x[g * 8 : (g + 1) * 8] for g in range(4)], 1)
    stacked = jnp.concatenate([p.astype(F32) for p in split(coeff)], 0).astype(BF16)
    response = jnp.zeros(coeff.shape, F32)
    owner = rows(coeff.shape) >> 1
    for i in range(4):
        a = dot(stacked, high[i], NT)
        b = dot(stacked, low[i], NT)
        response = jnp.where(owner == i, a[0:8] + (a[8:16] + b[0:8]), response)
    y = jnp.concatenate([response[:, g * 128 : (g + 1) * 128] for g in range(4)], 0)
    y = block_transpose(y, 16)
    for r in range(8):
        message[r * 32 : (r + 1) * 32, :] = y


def apply_wall(arrived, high, low):
    return pl.pallas_call(
        wall_kernel,
        out_shape=jax.ShapeDtypeStruct(arrived.shape, F32),
        in_specs=[VMEM, VMEM, VMEM],
        out_specs=VMEM,
        compiler_params=params(8),
        cost_estimate=cost(3 * 2 * 16 * 512 * 512 * 4, 4 << 20),
        name="wall",
    )(arrived, high, low)


def pack_kernel(mag, vel, left, right, bottom, top):
    nz, nr, cells = mag.shape[1:]
    lane = lanes((8, cells))
    for f in range(6):
        ref = mag if f < 3 else vel
        bottom[f] = ref[f % 3, 0]
        top[f] = ref[f % 3, nz - 1]

        def body(z, carry, ref=ref, f=f):
            low, high = carry
            for t in range(8):
                j = z * 8 + t
                tile = pltpu.roll(ref[f % 3, z, t * 8 : (t + 1) * 8, :], j, 1)
                low = jnp.where(lane == j, tile, low)
                high = jnp.where(lane == ((j + 127) & 127), tile, high)
            return low, high

        zero = jnp.zeros((8, cells), F32)
        low, high = lax.fori_loop(0, nz, body, (zero, zero))
        left[f] = low
        right[f] = high


def pack(mag, vel):
    nz, nr, cells = mag.shape[1:]
    edge = jax.ShapeDtypeStruct((6, 8, cells), F32)
    layer = jax.ShapeDtypeStruct((6, nr, cells), F32)
    return pl.pallas_call(
        pack_kernel,
        out_shape=(edge, edge, layer, layer),
        in_specs=[VMEM, VMEM],
        out_specs=(VMEM,) * 4,
        compiler_params=params(12),
        cost_estimate=cost(8 << 20, 4 << 20),
        name="pack",
    )(mag, vel)


def stencil_kernel(mag, vel, before, after, below, above, out, edge, pad_b, pad_u):
    nz, nr, cells = mag.shape[1:]
    lane = lanes((8, cells))
    row = rows((8, cells))
    inv_radial = 1.0 / (2.0 * RADIAL_STEP)
    inv_axial = 1.0 / (2.0 * AXIAL_STEP)
    angle_step = 2.0 * math.pi / (cells * 8)

    def body(z, _):
        for t in range(nr // 8):
            index = (t * 8 + row).astype(F32)
            radius = 1.0 - (nr - index - 0.5) * RADIAL_STEP
            inv_azimuth = 1.0 / (2.0 * radius * angle_step)
            inv_radius = 1.0 / radius
            second = 1.0 / (radius * angle_step) ** 2
            j = z * 8 + t
            grads = []
            centers = []
            extra = []
            for f in range(6):
                ref, pad, c = (mag, pad_b, f) if f < 3 else (vel, pad_u, f - 3)
                x = ref[c, z, t * 8 : (t + 1) * 8, :]
                outer = ref[c, z, min(t * 8 + 8, nr - 1) : min(t * 8 + 8, nr - 1) + 1, :]
                inner = ref[c, z, max(t * 8 - 1, 0) : max(t * 8 - 1, 0) + 1, :]
                r_next = jnp.where(row == 7, outer, pltpu.roll(x, 7, 0))
                r_prev = jnp.where(row == 0, inner, pltpu.roll(x, 1, 0))
                h_next = pltpu.roll(after[f], (255 - j) & 127, 1)
                h_prev = pltpu.roll(before[f], (129 - j) & 127, 1)
                p_next = jnp.where(lane == cells - 1, h_next, pltpu.roll(x, cells - 1, 1))
                p_prev = jnp.where(lane == 0, h_prev, pltpu.roll(x, 1, 1))
                z_next = pad[c, z + 2, t * 8 : (t + 1) * 8, :]
                z_prev = pad[c, z, t * 8 : (t + 1) * 8, :]
                centers.append(x)
                grads.append(
                    (
                        (r_next - r_prev) * inv_radial,
                        (p_next - p_prev) * inv_azimuth,
                        (z_next - z_prev) * inv_axial,
                    )
                )
                if f < 3:
                    twice = 2.0 * x
                    laplace = (r_next - twice + r_prev) * (1.0 / RADIAL_STEP**2)
                    laplace = laplace + grads[f][0] * inv_radius
                    laplace = laplace + (p_next - twice + p_prev) * second
                    laplace = laplace + (z_next - twice + z_prev) * (1.0 / AXIAL_STEP**2)
                    extra.append(laplace)
            for c in range(3):
                gb, gu = grads[c], grads[c + 3]
                carried = centers[3] * gb[0] + centers[4] * gb[1] + centers[5] * gb[2]
                stretched = centers[0] * gu[0] + centers[1] * gu[1] + centers[2] * gu[2]
                value = centers[c] + TIME_STEP * (DIFFUSIVITY * extra[c] - carried + stretched)
                out[c, z, t * 8 : (t + 1) * 8, :] = value
                if c and t == nr // 8 - 1:
                    edge[c - 1, z] = value
            if t == nr // 8 - 1:
                last = 1.0 - 0.5 * RADIAL_STEP
                fixed = TIME_STEP * DIFFUSIVITY * (1.0 / RADIAL_STEP**2 + inv_radial / last)
                edge[2, z] = fixed - (TIME_STEP * inv_radial) * centers[3]
        return 0

    for f in range(6):
        ref, pad, c = (mag, pad_b, f) if f < 3 else (vel, pad_u, f - 3)
        pad[c, 0] = below[f]
        pad[c, nz + 1] = above[f]
        pad[c, 1 : nz + 1] = ref[c]
    lax.fori_loop(0, nz, body, 0)


def stencil(mag, vel, before, after, below, above):
    nz, nr, cells = mag.shape[1:]
    return pl.pallas_call(
        stencil_kernel,
        out_shape=(
            jax.ShapeDtypeStruct(mag.shape, F32),
            jax.ShapeDtypeStruct((3, nz, 8, cells), F32),
        ),
        in_specs=[VMEM] * 6,
        out_specs=(VMEM, VMEM),
        scratch_shapes=[
            pltpu.VMEM((3, nz + 2, nr, cells), F32),
            pltpu.VMEM((3, nz + 2, nr, cells), F32),
        ],
        compiler_params=params(20),
        cost_estimate=cost(40 << 20, 8 << 20),
        name="stencil",
    )(mag, vel, before, after, below, above)


def decode_kernel(arrived, high, low, layers, edge, held, flux, out, fixed, sem):
    del held
    nz, cells = flux.shape[1:]
    turned = jnp.transpose(arrived[...], (1, 0))
    th, tl = split(turned)
    total = jnp.zeros((2 * nz, cells), F32)
    for i in range(4):
        part = slice(i * 2 * nz, (i + 1) * 2 * nz)
        total = total + dot3((th[part], tl[part]), (high[i], low[i]), NN)
    total = total.reshape(2, nz, cells)
    flux[...] = total
    thickness = layers[...].astype(F32) * (1.0 / LW)
    row = rows((nz, 8, cells))
    for c in range(2):
        change = (thickness * total[c])[:, None, :] * edge[2]
        fixed[c] = edge[c] - jnp.where(row == 7, change, 0.0)
    copy = pltpu.make_async_copy(fixed, out.at[1:3, :, 56:64, :], sem)
    copy.start()
    copy.wait()


def decode(arrived, high, low, layers, edge, held):
    nz, nr, cells = held.shape[1:]
    return pl.pallas_call(
        decode_kernel,
        out_shape=(
            jax.ShapeDtypeStruct((2, nz, cells), F32),
            jax.ShapeDtypeStruct(held.shape, F32),
        ),
        in_specs=[VMEM] * 5 + [ANY],
        out_specs=(VMEM, ANY),
        scratch_shapes=[pltpu.VMEM((2, nz, 8, cells), F32), pltpu.SemaphoreType.DMA],
        input_output_aliases={5: 1},
        compiler_params=params(8),
        cost_estimate=cost(12 << 20, 1 << 20),
        name="decode",
    )(arrived, high, low, layers.reshape(1, cells), edge, held)


def neighbours(low, high, axis, periodic):
    count = lax.axis_size(axis)
    forward = [(i, i + 1) for i in range(count - 1)]
    if periodic:
        forward.append((count - 1, 0))
    backward = [(target, source) for source, target in forward]
    return lax.ppermute(high, axis, forward), lax.ppermute(low, axis, backward)


def shards(magnetic, velocity, wall_response, mode_slots, wall_layers):
    message, table = encode(magnetic, mode_slots)
    arrived = lax.all_to_all(message, BOTH, 0, 0, tiled=True)
    left, right, bottom, top = pack(magnetic, velocity)
    before, after = neighbours(left, right, "region", True)
    below, above = neighbours(bottom, top, "slab", False)
    wall_high, wall_low = halves(wall_response)
    table_high, table_low = weigh(table, mode_slots)
    replies = apply_wall(arrived, wall_high, wall_low)
    returned = lax.all_to_all(replies, BOTH, 0, 0, tiled=True)
    stepped, edge = stencil(magnetic, velocity, before, after, below, above)
    wall_flux, magnetic_next = decode(
        returned, table_high, table_low, wall_layers, edge, stepped
    )
    return magnetic_next, wall_flux


def solution(mesh):
    placed = (
        P(None, "slab", None, "region"),
        P(None, "slab", None, "region"),
        P(BOTH, None, None),
        P(),
        P("region"),
    )
    return jax.shard_map(
        shards,
        mesh=mesh,
        in_specs=placed,
        out_specs=(P(None, "slab", None, "region"), P(None, "slab", "region")),
        check_vma=False,
    )
```

time: 232 us -> 81.1 us (0.35)
  the two profiles are of different devices: /device:TPU:2 before, /device:TPU:71 now
where the time goes in v1:
time: 81.1 us; the launch traced here: 80.7 us
  starting transfers between devices  36 us (44%)
  Pallas kernels  19.9 us (25%)
  local copies, waits for them, and re-layouts  14.2 us (18%)
  waiting for transfers between devices  9.89 us (12%)
    all_to_all x1, starting transfers between devices, shards(): arrived = lax.all_to_all(message, BOTH, 0, 0, tiled=True)  14.5 us
    unnamed x34, local copies, waits for them, and re-layouts  14.2 us
    all_to_all x1, starting transfers between devices, shards(): returned = lax.all_to_all(replies, BOTH, 0, 0, tiled=True)  9.97 us
    pallas_call x1, Pallas kernels, pack(): pl.pallas_call(pack_kernel, out_shape=(edge, edge, layer, layer), in_spec...  7.33 us
    ppermute x2, starting transfers between devices, neighbours(): lax.ppermute(high, axis, forward)  6.56 us
    ppermute x2, waiting for transfers between devices, neighbours(): lax.ppermute(low, axis, backward)  6.01 us
    pallas_call x1, Pallas kernels, stencil(): pl.pallas_call(stencil_kernel, out_shape=(jax.ShapeDtypeStruct(mag.shape,...  5.88 us
    ppermute x2, starting transfers between devices, neighbours(): lax.ppermute(low, axis, backward)  4.94 us
  transfers between devices with their start and end apart: 6, of which 3 were waited for; matrix products, arithmetic and copies ran while one was open for 0% of the time, Pallas kernels for 18%

profile of v1, /device:TPU:71, one launch (start us, length us, event | category | flops | bytes accessed | tf_op | source)
XLA Modules:
  0.0 80.7 jit_solution(731827476024434347)
XLA Ops:
  0.6 0.0 copy-start
  0.6 1.4 %copy-done = f32[3,16,64,128]{3,2,1,0:T(8,128)S(1)} copy-done((f32[3,16,64,128]{3,2,1,0:T(8,128)S(1)}, f32[3,16,64,128]{3,2,1,0:T(8,128)}, u32[]{:S(2)}) %copy-start) | copy-done | bytes 1572888
  2.0 0.0 copy-start.14
  2.0 0.7 copy-done.14
  2.7 1.9 %encode.1 = (f32[256,128]{1,0:T(8,128)}, f32[1024,128]{1,0:T(8,128)S(1)}) custom-call(f32[3,16,64,128]{3,2,1,0:T(8,128)S(1)} %copy-done, s32[8,128]{1,0:T(8,128)S(1)} %bitcast.12), custom_call_target="tpu_custom_call" | custom-call | flops 100663296 | bytes 1048576 | tf_op jit(solution)/shard_map/encode/pallas_call | solution.py:108
  4.6 0.0 copy-start.8
  4.6 0.8 copy-done.8
  5.4 14.5 %all-to-all-start = ((f32[256,1,128]{2,1,0:T(1,128)}), f32[256,1,128]{2,1,0:T(1,128)S(1)}, u32[]{:S(2)}, u32[]{:S(2)}) async-start(f32[256,1,128]{2,1,0:T(1,128)} %bitcast.2), calls=%async_computation | async-start | bytes 262144 | tf_op jit(solution)/shard_map/all_to_all | solution.py:381
  19.9 0.0 copy-start.3
  19.9 2.2 %copy-done.3 = f32[4,512,512]{2,1,0:T(8,128)S(1)} copy-done((f32[4,512,512]{2,1,0:T(8,128)S(1)}, f32[4,512,512]{2,1,0:T(8,128)}, u32[]{:S(2)}) %copy-start.3) | copy-done | bytes 4194328
  22.1 0.6 halves.1
  22.7 0.0 copy-start.4
  22.7 1.3 %copy-done.4 = bf16[4,512,512]{2,1,0:T(8,128)(2,1)} copy-done((bf16[4,512,512]{2,1,0:T(8,128)(2,1)}, bf16[4,512,512]{2,1,0:T(8,128)(2,1)S(1)}, u32[]{:S(2)}) %copy-start.4) | copy-done | bytes 2097176
  24.1 0.0 copy-start.6
  24.1 1.3 %copy-done.6 = bf16[4,512,512]{2,1,0:T(8,128)(2,1)} copy-done((bf16[4,512,512]{2,1,0:T(8,128)(2,1)}, bf16[4,512,512]{2,1,0:T(8,128)(2,1)S(1)}, u32[]{:S(2)}) %copy-start.6) | copy-done | bytes 2097176
  25.4 3.7 %all-to-all-done = f32[256,1,128]{2,1,0:T(1,128)S(1)} async-done(((f32[256,1,128]{2,1,0:T(1,128)}), f32[256,1,128]{2,1,0:T(1,128)S(1)}, u32[]{:S(2)}, u32[]{:S(2)}) %all-to-all-start) | async-done | bytes 131104 | tf_op jit(solution)/shard_map/all_to_all | solution.py:381
  29.1 0.0 copy-start.5
  29.1 1.6 %copy-done.5 = bf16[4,512,512]{2,1,0:T(8,128)(2,1)S(1)} copy-done((bf16[4,512,512]{2,1,0:T(8,128)(2,1)S(1)}, bf16[4,512,512]{2,1,0:T(8,128)(2,1)}, u32[]{:S(2)}) %copy-start.5) | copy-done | bytes 2097176
  30.7 0.0 copy-start.7
  30.7 1.6 %copy-done.7 = bf16[4,512,512]{2,1,0:T(8,128)(2,1)S(1)} copy-done((bf16[4,512,512]{2,1,0:T(8,128)(2,1)S(1)}, bf16[4,512,512]{2,1,0:T(8,128)(2,1)}, u32[]{:S(2)}) %copy-start.7) | copy-done | bytes 2097176
  32.3 0.0 copy-start.1
  32.3 2.3 %wall.3 = f32[256,128]{1,0:T(8,128)} custom-call(f32[256,128]{1,0:T(8,128)S(1)} %bitcast.10, bf16[4,512,512]{2,1,0:T(8,128)(2,1)S(1)} %copy-done.5, bf16[4,512,512]{2,1,0:T(8,128)(2,1)S(1)} %copy-done.7), custom_call_target="tpu_custom_call" | custom-call | flops 100663296 | bytes 4194304 | tf_op jit(solution)/shard_map/wall/pallas_call | solution.py:193
  34.6 10.0 %all-to-all-start.1 = ((f32[256,1,128]{2,1,0:T(1,128)}), f32[256,1,128]{2,1,0:T(1,128)S(1)}, u32[]{:S(2)}, u32[]{:S(2)}) async-start(f32[256,1,128]{2,1,0:T(1,128)} %bitcast.5), calls=%async_computation.1 | async-start | bytes 262144 | tf_op jit(solution)/shard_map/all_to_all | solution.py:388
  44.5 0.0 copy-done.1
  44.5 0.0 copy-done.2
  44.5 0.0 copy-start.9
  44.6 0.0 copy-start.15
  44.6 7.3 %pack.1 = (f32[6,8,128]{2,1,0:T(8,128)S(1)}, f32[6,8,128]{2,1,0:T(8,128)S(1)}, f32[6,64,128]{2,1,0:T(8,128)S(1)}, f32[6,64,128]{2,1,0:T(8,128)S(1)}) custom-call(f32[3,16,64,128]{3,2,1,0:T(8,128)S(1)} %copy-done.1, f32[3,16,64,128]{3,2,1,0:T(8,128)S(1)} %copy-done.2), custom_call_target="tpu_custom_call" | custom-call | flops 8388608 | bytes 4194304 | tf_op jit(solution)/shard_map/pack/pallas_call | solution.py:231
  51.9 5.9 %collective-permute-start.2 = (f32[6,64,128]{2,1,0:T(8,128)S(1)}, f32[6,64,128]{2,1,0:T(8,128)S(1)}, u32[]{:S(2)}, u32[]{:S(2)}) collective-permute-start(f32[6,64,128]{2,1,0:T(8,128)S(1)} %get-tuple-element.24), channel_id=1, source_target_pairs={{0,1},{1,2},{2,3},{3,4},{4,5},{5,6},{6,7},{7,8},{8,9},{9,10},{10,1... | collective-permute-start | bytes 589832 | tf_op jit(solution)/shard_map/ppermute | solution.py:376
  57.8 1.9 %collective-permute-start.3 = (f32[6,64,128]{2,1,0:T(8,128)S(1)}, f32[6,64,128]{2,1,0:T(8,128)S(1)}, u32[]{:S(2)}, u32[]{:S(2)}) collective-permute-start(f32[6,64,128]{2,1,0:T(8,128)S(1)} %get-tuple-element.25), channel_id=1, source_target_pairs={{1,0},{2,1},{3,2},{4,3},{5,4},{6,5},{7,6},{8,7},{9,8},{10,9},{11,1... | collective-permute-start | bytes 589832 | tf_op jit(solution)/shard_map/ppermute | solution.py:376
  59.8 0.6 collective-permute-start
  60.4 3.0 %collective-permute-start.1 = (f32[6,8,128]{2,1,0:T(8,128)S(1)}, f32[6,8,128]{2,1,0:T(8,128)S(1)}, u32[]{:S(2)}, u32[]{:S(2)}) collective-permute-start(f32[6,8,128]{2,1,0:T(8,128)S(1)} %get-tuple-element.23), channel_id=1, source_target_pairs={{32,0},{64,32},{96,64},{128,96},{160,128},{192,160},{224,192},{0,2... | collective-permute-start | bytes 73736 | tf_op jit(solution)/shard_map/ppermute | solution.py:376
  63.4 0.0 copy-done.9
  63.4 0.0 copy-done.15
  63.4 0.4 weigh.1
  63.8 0.0 copy-start.10
  63.8 0.7 copy-done.10
  64.5 0.1 collective-permute-done.before
  64.6 0.0 collective-permute-done.1.after
  64.6 0.0 collective-permute-done.2.below
  64.6 6.0 %collective-permute-done.3.above = f32[6,64,128]{2,1,0:T(8,128)S(1)} collective-permute-done((f32[6,64,128]{2,1,0:T(8,128)S(1)}, f32[6,64,128]{2,1,0:T(8,128)S(1)}, u32[]{:S(2)}, u32[]{:S(2)}) %collective-permute-start.3) | collective-permute-done | bytes 196640 | tf_op jit(solution)/shard_map/ppermute | solution.py:376
  70.7 5.9 %stencil.1 = (f32[3,16,64,128]{3,2,1,0:T(8,128)}, f32[3,16,8,128]{3,2,1,0:T(8,128)S(1)}) custom-call(f32[3,16,64,128]{3,2,1,0:T(8,128)S(1)} %copy-done.1, f32[3,16,64,128]{3,2,1,0:T(8,128)S(1)} %copy-done.2, f32[6,8,128]{2,1,0:T(8,128)S(1)} %collective-permute-done.before, f32[6,8,128]{2,1,0:T(8,128)S(1)} %collective-permute-done.1.after, ...), custom_call_target="tpu_custom_call" | custom-call | flops 41943040 | bytes 8388608 | tf_op jit(solution)/shard_map/stencil/pallas_call | solution.py:313
  76.5 0.7 copy-done.12
  77.2 0.0 all-to-all-done.1
  77.2 0.0 copy-done.16
  77.2 0.9 %copy-done.11 = bf16[4,256,128]{2,1,0:T(8,128)(2,1)S(1)} copy-done((bf16[4,256,128]{2,1,0:T(8,128)(2,1)S(1)}, bf16[4,256,128]{2,1,0:T(8,128)(2,1)}, u32[]{:S(2)}) %copy-start.11) | copy-done | bytes 262168
  78.2 0.9 %copy-done.13 = f32[3,16,8,128]{3,2,1,0:T(8,128)S(1)} copy-done((f32[3,16,8,128]{3,2,1,0:T(8,128)S(1)}, f32[3,16,8,128]{3,2,1,0:T(8,128)}, u32[]{:S(2)}) %copy-start.13) | copy-done | bytes 196632
  79.1 1.6 %decode.1 = (f32[2,16,128]{2,1,0:T(8,128)}, f32[3,16,64,128]{3,2,1,0:T(8,128)}) custom-call(f32[256,128]{1,0:T(8,128)S(1)} %bitcast.11, bf16[4,256,128]{2,1,0:T(8,128)(2,1)S(1)} %get-tuple-element.20.high, bf16[4,256,128]{2,1,0:T(8,128)(2,1)S(1)} %copy-done.11, s32[1,128]{1,0:T(1,128)S(1)} %bitcast.14, ...), custom_call_target="tpu_custom_call", output_to_operand_aliasing={{1}: (5, {})} | custom-call | flops 12582912 | bytes 1048576 | tf_op jit(solution)/shard_map/decode/pallas_call | solution.py:354
  (5 shorter events, 0.0 us)
Async XLA Ops:
  0.6 1.4 %copy-start = (f32[3,16,64,128]{3,2,1,0:T(8,128)S(1)}, f32[3,16,64,128]{3,2,1,0:T(8,128)}, u32[]{:S(2)}) copy-start(f32[3,16,64,128]{3,2,1,0:T(8,128)} %mag.5) | copy-start | bytes 4718596
  2.0 0.7 copy-start.14
  4.6 0.8 copy-start.8
  5.4 23.7 %all-to-all-start = ((f32[256,1,128]{2,1,0:T(1,128)}), f32[256,1,128]{2,1,0:T(1,128)S(1)}, u32[]{:S(2)}, u32[]{:S(2)}) async-start(f32[256,1,128]{2,1,0:T(1,128)} %bitcast.2), calls=%async_computation | async-start | bytes 262144 | tf_op jit(solution)/shard_map/all_to_all | solution.py:381
  19.9 2.2 %copy-start.3 = (f32[4,512,512]{2,1,0:T(8,128)S(1)}, f32[4,512,512]{2,1,0:T(8,128)}, u32[]{:S(2)}) copy-start(f32[4,512,512]{2,1,0:T(8,128)} %wall.2) | copy-start | bytes 12582916
  22.7 1.4 %copy-start.4 = (bf16[4,512,512]{2,1,0:T(8,128)(2,1)}, bf16[4,512,512]{2,1,0:T(8,128)(2,1)S(1)}, u32[]{:S(2)}) copy-start(bf16[4,512,512]{2,1,0:T(8,128)(2,1)S(1)} %get-tuple-element.17.high) | copy-start | bytes 6291460
  24.1 1.3 %copy-start.6 = (bf16[4,512,512]{2,1,0:T(8,128)(2,1)}, bf16[4,512,512]{2,1,0:T(8,128)(2,1)S(1)}, u32[]{:S(2)}) copy-start(bf16[4,512,512]{2,1,0:T(8,128)(2,1)S(1)} %get-tuple-element.18.low) | copy-start | bytes 6291460
  29.1 1.6 %copy-start.5 = (bf16[4,512,512]{2,1,0:T(8,128)(2,1)S(1)}, bf16[4,512,512]{2,1,0:T(8,128)(2,1)}, u32[]{:S(2)}) copy-start(bf16[4,512,512]{2,1,0:T(8,128)(2,1)} %copy-done.4) | copy-start | bytes 6291460
  30.7 1.6 %copy-start.7 = (bf16[4,512,512]{2,1,0:T(8,128)(2,1)S(1)}, bf16[4,512,512]{2,1,0:T(8,128)(2,1)}, u32[]{:S(2)}) copy-start(bf16[4,512,512]{2,1,0:T(8,128)(2,1)} %copy-done.6) | copy-start | bytes 6291460
  32.3 12.2 %copy-start.1 = (f32[3,16,64,128]{3,2,1,0:T(8,128)S(1)}, f32[3,16,64,128]{3,2,1,0:T(8,128)}, u32[]{:S(2)}) copy-start(f32[3,16,64,128]{3,2,1,0:T(8,128)} %mag.5) | copy-start | bytes 4718596
  32.3 12.3 %copy-start.2 = (f32[3,16,64,128]{3,2,1,0:T(8,128)S(1)}, f32[3,16,64,128]{3,2,1,0:T(8,128)}, u32[]{:S(2)}) copy-start(f32[3,16,64,128]{3,2,1,0:T(8,128)} %vel.3) | copy-start | bytes 4718596
  34.6 42.7 %all-to-all-start.1 = ((f32[256,1,128]{2,1,0:T(1,128)}), f32[256,1,128]{2,1,0:T(1,128)S(1)}, u32[]{:S(2)}, u32[]{:S(2)}) async-start(f32[256,1,128]{2,1,0:T(1,128)} %bitcast.5), calls=%async_computation.1 | async-start | bytes 262144 | tf_op jit(solution)/shard_map/all_to_all | solution.py:388
  44.5 18.9 %copy-start.9 = (f32[1024,128]{1,0:T(8,128)S(1)}, f32[1024,128]{1,0:T(8,128)}, u32[]{:S(2)}) copy-start(f32[1024,128]{1,0:T(8,128)} %copy-done.8) | copy-start | bytes 1572868
  44.6 18.9 %copy-start.15 = (s32[1024]{0:T(1024)S(1)}, s32[1024]{0:T(1024)}, u32[]{:S(2)}) copy-start(s32[1024]{0:T(1024)} %param.8) | copy-start | bytes 12292
  51.9 12.7 %collective-permute-start.2 = (f32[6,64,128]{2,1,0:T(8,128)S(1)}, f32[6,64,128]{2,1,0:T(8,128)S(1)}, u32[]{:S(2)}, u32[]{:S(2)}) collective-permute-start(f32[6,64,128]{2,1,0:T(8,128)S(1)} %get-tuple-element.24), channel_id=1, source_target_pairs={{0,1},{1,2},{2,3},{3,4},{4,5},{5,6},{6,7},{7,8},{8,9},{9,10},{10,1... | collective-permute-start | bytes 589832 | tf_op jit(solution)/shard_map/ppermute | solution.py:376
  57.8 12.8 %collective-permute-start.3 = (f32[6,64,128]{2,1,0:T(8,128)S(1)}, f32[6,64,128]{2,1,0:T(8,128)S(1)}, u32[]{:S(2)}, u32[]{:S(2)}) collective-permute-start(f32[6,64,128]{2,1,0:T(8,128)S(1)} %get-tuple-element.25), channel_id=1, source_target_pairs={{1,0},{2,1},{3,2},{4,3},{5,4},{6,5},{7,6},{8,7},{9,8},{10,9},{11,1... | collective-permute-start | bytes 589832 | tf_op jit(solution)/shard_map/ppermute | solution.py:376
  59.8 4.9 %collective-permute-start = (f32[6,8,128]{2,1,0:T(8,128)S(1)}, f32[6,8,128]{2,1,0:T(8,128)S(1)}, u32[]{:S(2)}, u32[]{:S(2)}) collective-permute-start(f32[6,8,128]{2,1,0:T(8,128)S(1)} %get-tuple-element.22), channel_id=1, source_target_pairs={{0,32},{32,64},{64,96},{96,128},{128,160},{160,192},{192,224},{224... | collective-permute-start | bytes 73736 | tf_op jit(solution)/shard_map/ppermute | solution.py:376
  60.4 4.2 %collective-permute-start.1 = (f32[6,8,128]{2,1,0:T(8,128)S(1)}, f32[6,8,128]{2,1,0:T(8,128)S(1)}, u32[]{:S(2)}, u32[]{:S(2)}) collective-permute-start(f32[6,8,128]{2,1,0:T(8,128)S(1)} %get-tuple-element.23), channel_id=1, source_target_pairs={{32,0},{64,32},{96,64},{128,96},{160,128},{192,160},{224,192},{0,2... | collective-permute-start | bytes 73736 | tf_op jit(solution)/shard_map/ppermute | solution.py:376
  63.8 0.7 copy-start.10
  64.5 12.7 %copy-start.16 = (s32[128]{0:T(128)S(1)}, s32[128]{0:T(128)}, u32[]{:S(2)}) copy-start(s32[128]{0:T(128)} %param.9) | copy-start | bytes 1540
  76.5 0.7 copy-start.12
  77.2 1.0 %copy-start.11 = (bf16[4,256,128]{2,1,0:T(8,128)(2,1)S(1)}, bf16[4,256,128]{2,1,0:T(8,128)(2,1)}, u32[]{:S(2)}) copy-start(bf16[4,256,128]{2,1,0:T(8,128)(2,1)} %copy-done.10) | copy-start | bytes 786436
  78.2 0.9 %copy-start.13 = (f32[3,16,8,128]{3,2,1,0:T(8,128)S(1)}, f32[3,16,8,128]{3,2,1,0:T(8,128)}, u32[]{:S(2)}) copy-start(f32[3,16,8,128]{3,2,1,0:T(8,128)} %copy-done.12) | copy-start | bytes 589828

commit v2 on v1

v2 whole, which is shorter than its diff:
```python
import math

import jax
import jax.numpy as jnp
from jax import lax
from jax.experimental import pallas as pl
from jax.experimental.pallas import tpu as pltpu
from jax.sharding import PartitionSpec as P

LW = 8
TIME_STEP = 0.0003
DIFFUSIVITY = 0.001
RADIAL_STEP = 1.0 / 384.0
AXIAL_STEP = 1.0 / 768.0

F32 = jnp.float32
BF16 = jnp.bfloat16
BOTH = ("region", "slab")
VMEM = pl.BlockSpec(memory_space=pltpu.VMEM)
ANY = pl.BlockSpec(memory_space=pl.ANY)
HBM = pl.BlockSpec(memory_space=pltpu.HBM)
NT = (((1,), (1,)), ((), ()))
NN = (((1,), (0,)), ((), ()))


def pinned(*arrays):
    return [pltpu.with_memory_space_constraint(a, pltpu.HBM) for a in arrays]


def params(mib):
    return pltpu.CompilerParams(vmem_limit_bytes=mib * 1024 * 1024)


def cost(flops, nbytes):
    return pl.CostEstimate(flops=flops, bytes_accessed=nbytes, transcendentals=0)


def lanes(shape):
    return lax.broadcasted_iota(jnp.int32, shape, len(shape) - 1)


def rows(shape):
    return lax.broadcasted_iota(jnp.int32, shape, len(shape) - 2)


def split(x):
    high = x.astype(BF16)
    return high, (x - high.astype(F32)).astype(BF16)


def dot(a, b, dims):
    return lax.dot_general(a, b, dims, preferred_element_type=F32)


def half_turn_sine(phase, total):
    half = phase - total
    fold = jnp.abs(half)
    fold = jnp.minimum(fold, total - fold)
    x = fold.astype(F32) * (math.pi / total)
    y = x * x
    poly = -1.0 / math.factorial(11)
    for n, sign in ((9, 1.0), (7, -1.0), (5, 1.0), (3, -1.0)):
        poly = poly * y + sign / math.factorial(n)
    value = x + x * (y * poly)
    return jnp.where(half < 0, value, -value)


def block_transpose(x, width):
    r, b = rows(x.shape), lanes(x.shape) // width
    n, m = x.shape
    for bit in range(3):
        h = 1 << bit
        down = pltpu.roll(pltpu.roll(x, h, 0), m - width * h, 1)
        up = pltpu.roll(pltpu.roll(x, n - h, 0), width * h, 1)
        rb, bb = (r >> bit) & 1, (b >> bit) & 1
        x = jnp.where(rb == bb, x, jnp.where(rb == 1, down, up))
    return x


def encode_kernel(mag, modes, message, table, edge, slots, turned, parts, sems):
    count, cells = parts.shape[1], edge.shape[3]
    nmodes = 4 * count
    get_modes = pltpu.make_async_copy(modes, slots, sems.at[0])
    get_edge = pltpu.make_async_copy(mag.at[1:3, :, 56:64, :], edge, sems.at[1])
    get_modes.start()
    get_edge.start()
    first = lax.axis_index("region") * cells
    odd_cell = (2 * (first + lanes((cells, cells))) + 1).astype(F32)
    get_modes.wait()
    filler = jnp.zeros((120, 128), F32)
    turned[...] = jnp.transpose(jnp.concatenate([slots[...].astype(F32), filler], 0), (1, 0))
    for i in range(4):
        strip = turned[pl.ds(i, 32, stride=4), :]
        for half in range(count // 128):
            columns = [strip[:, half * 4 + q : half * 4 + q + 1] for q in range(4)]
            mode = jnp.concatenate([jnp.broadcast_to(c, (32, cells)) for c in columns], 0)
            mode = mode.astype(jnp.int32)
            phase = (((mode + 1) >> 1).astype(F32) * odd_cell).astype(jnp.int32)
            phase = jnp.where((mode & 1) == 1, phase, phase + nmodes // 2) & (2 * nmodes - 1)
            high, low = split(half_turn_sine(phase, nmodes))
            part = slice(half * 128, half * 128 + 128)
            parts[i, part, 0:cells] = high
            parts[i, part, cells : 2 * cells] = low
    put_table = pltpu.make_async_copy(parts, table, sems.at[2])
    put_table.start()
    get_edge.wait()
    trace = edge[:, :, 7, :].reshape(32, cells)
    high, low = split(jnp.concatenate([trace] * 4, 0))
    weights = jnp.concatenate([jnp.concatenate([p, p], 1) for p in (high, low)], 0)
    lane = lanes((count, 128)) // 32
    out = jnp.zeros((count, 128), F32)
    for i in range(4):
        strip = turned[pl.ds(i, 32, stride=4), :]
        single = (strip == 0.0) | (strip == float(nmodes - 1))
        strip = jnp.where(single, 1.0 / nmodes, 2.0 / nmodes)
        scale = [jnp.broadcast_to(strip[:, r : r + 1], (32, 128)) for r in range(count // 32)]
        both = dot(parts[i], weights, NT)
        both = (both[:, 0:128] + both[:, 128:256]) * jnp.concatenate(scale, 0)
        out = jnp.where(lane == i, both, out)
    message[...] = out
    put_table.wait()


def encode(mag, modes):
    nz, _, cells = mag.shape[1:]
    count = modes.size // 4
    return pl.pallas_call(
        encode_kernel,
        out_shape=(
            jax.ShapeDtypeStruct((count, 128), F32),
            pltpu.HBM((4, count, 2 * cells), BF16),
        ),
        in_specs=[HBM, HBM],
        out_specs=(VMEM, HBM),
        scratch_shapes=[
            pltpu.VMEM((2, nz, 8, cells), F32),
            pltpu.VMEM((8, 128), jnp.int32),
            pltpu.VMEM((128, 128), F32),
            pltpu.VMEM((4, count, 2 * cells), BF16),
            pltpu.SemaphoreType.DMA((3,)),
        ],
        compiler_params=params(8),
        cost_estimate=cost(3 * 2 * 1024 * 128 * 128, 1 << 20),
        name="encode",
    )(*pinned(mag, modes.reshape(8, 128)))


def wall_kernel(arrived, wall, *rest):
    message, held, sems = rest[-3:]
    copies = [pltpu.make_async_copy(wall.at[i], held.at[i], sems.at[i]) for i in range(4)]
    for copy in copies:
        copy.start()
    x = arrived[0:32, :]
    for r in range(1, 8):
        x = x + arrived[r * 32 : (r + 1) * 32, :]
    x = block_transpose(x, 16)
    coeff = jnp.concatenate([x[g * 8 : (g + 1) * 8] for g in range(4)], 1)
    stacked = jnp.concatenate([p.astype(F32) for p in split(coeff)], 0).astype(BF16)
    response = jnp.zeros(coeff.shape, F32)
    owner = rows(coeff.shape) >> 1
    for i in range(4):
        copies[i].wait()
        high, low = split(held[i])
        a = dot(stacked, high, NT)
        b = dot(stacked, low, NT)
        response = jnp.where(owner == i, a[0:8] + (a[8:16] + b[0:8]), response)
    y = jnp.concatenate([response[:, g * 128 : (g + 1) * 128] for g in range(4)], 0)
    y = block_transpose(y, 16)
    for r in range(8):
        message[r * 32 : (r + 1) * 32, :] = y


def apply_wall(arrived, wall, *earlier):
    return pl.pallas_call(
        wall_kernel,
        out_shape=jax.ShapeDtypeStruct(arrived.shape, F32),
        in_specs=[VMEM, HBM] + [ANY] * len(earlier),
        out_specs=VMEM,
        scratch_shapes=[pltpu.VMEM(wall.shape, F32), pltpu.SemaphoreType.DMA((4,))],
        compiler_params=params(16),
        cost_estimate=cost(3 * 2 * 16 * 512 * 512 * 4, 4 << 20),
        name="wall",
    )(arrived, *pinned(wall), *earlier)


def fetch(mag, vel, held, sems):
    return [
        [
            pltpu.make_async_copy(
                ref.at[:, pl.ds(part * 4, 4)], held.at[k, :, pl.ds(part * 4, 4)], sems.at[k, part]
            )
            for k, ref in enumerate((mag, vel))
        ]
        for part in range(held.shape[2] // 4)
    ]


def pack_kernel(mag, vel, left, right, bottom, top, held, low_sems, high_sems, sems):
    nz, nr, cells = mag.shape[1:]
    lane = lanes((8, cells))
    copies = fetch(mag, vel, held, sems)
    for pair in copies:
        for copy in pair:
            copy.start()

    def body(z, carry):
        low, high = list(carry[0]), list(carry[1])
        for t in range(8):
            j = z * 8 + t
            here, wrapped = lane == j, lane == ((j + 127) & 127)
            for f in range(6):
                tile = pltpu.roll(held[f // 3, f % 3, z, t * 8 : (t + 1) * 8, :], j, 1)
                low[f] = jnp.where(here, tile, low[f])
                high[f] = jnp.where(wrapped, tile, high[f])
        return tuple(low), tuple(high)

    zero = (jnp.zeros((8, cells), F32),) * 6
    carry = (zero, zero)
    ends = []
    for part, pair in enumerate(copies):
        for copy in pair:
            copy.wait()
        for k in range(2):
            if part == 0:
                ends.append(pltpu.make_async_copy(held.at[k, :, 0], bottom.at[pl.ds(3 * k, 3)], low_sems.at[k]))
                ends[-1].start()
            if part == nz // 4 - 1:
                ends.append(pltpu.make_async_copy(held.at[k, :, nz - 1], top.at[pl.ds(3 * k, 3)], high_sems.at[k]))
                ends[-1].start()
        carry = lax.fori_loop(part * 4, part * 4 + 4, body, carry)
    for f in range(6):
        left[f] = carry[0][f]
        right[f] = carry[1][f]
    for copy in ends:
        copy.wait()


def pack(mag, vel):
    nz, nr, cells = mag.shape[1:]
    edge = jax.ShapeDtypeStruct((6, 8, cells), F32)
    return pl.pallas_call(
        pack_kernel,
        out_shape=(edge, edge, pltpu.HBM((6, nr, cells), F32), pltpu.HBM((6, nr, cells), F32)),
        in_specs=[HBM, HBM],
        out_specs=(VMEM, VMEM, HBM, HBM),
        scratch_shapes=[
            pltpu.VMEM((2, *mag.shape), F32),
            pltpu.SemaphoreType.DMA((2,)),
            pltpu.SemaphoreType.DMA((2,)),
            pltpu.SemaphoreType.DMA((2, nz // 4)),
        ],
        compiler_params=params(12),
        cost_estimate=cost(8 << 20, 4 << 20),
        name="pack",
    )(*pinned(mag, vel))


def stencil_kernel(mag, vel, before, after, below, above, out, held, stepped, factors, gets, sems):
    nz, nr, cells = mag.shape[1:]
    lane = lanes((8, cells))
    row = rows((8, cells))
    copies = fetch(mag, vel, held, gets)
    for pair in copies:
        for copy in pair:
            copy.start()
    angle_step = 2.0 * math.pi / (cells * 8)
    spread = TIME_STEP * DIFFUSIVITY
    by_radial = TIME_STEP / (2.0 * RADIAL_STEP)
    by_axial = TIME_STEP / (2.0 * AXIAL_STEP)
    second_radial = spread / RADIAL_STEP**2
    second_axial = spread / AXIAL_STEP**2
    for t in range(nr // 8):
        radius = 1.0 - (nr - (t * 8 + row).astype(F32) - 0.5) * RADIAL_STEP
        arc = 1.0 / (radius * angle_step)
        second = spread * arc * arc
        factors[0, t] = (0.5 * TIME_STEP) * arc
        factors[1, t] = (spread / (2.0 * RADIAL_STEP)) / radius
        factors[2, t] = second
        factors[3, t] = 1.0 - 2.0 * (second + (second_radial + second_axial))

    def layer(z, down, up):
        for t in range(nr // 8):
            j = z * 8 + t
            rows8 = slice(t * 8, t * 8 + 8)
            x, dr, dp, dz, sr, sp, sz = [], [], [], [], [], [], []
            for f in range(6):
                ref, c = held.at[f // 3], f % 3
                here = ref[c, z, rows8, :]
                if t == 0:
                    inner = jnp.where(row == 0, here, pltpu.roll(here, 1, 0))
                else:
                    inner = ref[c, z, t * 8 - 1 : t * 8 + 7, :]
                if t == nr // 8 - 1:
                    outer = jnp.where(row == 7, here, pltpu.roll(here, 7, 0))
                else:
                    outer = ref[c, z, t * 8 + 1 : t * 8 + 9, :]
                far = pltpu.roll(after[f], (255 - j) & 127, 1)
                near = pltpu.roll(before[f], (129 - j) & 127, 1)
                p_next = jnp.where(lane == cells - 1, far, pltpu.roll(here, cells - 1, 1))
                p_prev = jnp.where(lane == 0, near, pltpu.roll(here, 1, 1))
                z_next = up(f, rows8)
                z_prev = down(f, rows8)
                x.append(here)
                dr.append(outer - inner)
                dp.append(p_next - p_prev)
                dz.append(z_next - z_prev)
                if f < 3:
                    sr.append(outer + inner)
                    sp.append(p_next + p_prev)
                    sz.append(z_next + z_prev)
            turn, curve, second, keep = (factors[n, t] for n in range(4))
            ur = curve - by_radial * x[3]
            up_ = turn * x[4]
            uz = by_axial * x[5]
            br = by_radial * x[0]
            bp = turn * x[1]
            bz = by_axial * x[2]
            for c in range(3):
                value = keep * x[c] + second_radial * sr[c] + (second * sp[c] + second_axial * sz[c])
                value = value + (ur * dr[c] - up_ * dp[c]) - uz * dz[c]
                value = value + (br * dr[c + 3] + bp * dp[c + 3]) + bz * dz[c + 3]
                stepped[c, z, rows8, :] = value

    def inside(z, step):
        return lambda f, rows8: held[f // 3, f % 3, z + step, rows8, :]

    def send(part):
        return pltpu.make_async_copy(
            stepped.at[:, pl.ds(part * 4, 4)], out.at[:, pl.ds(part * 4, 4)], sems.at[part]
        )

    def body(z, _):
        layer(z, inside(z, -1), inside(z, 1))
        return 0

    parts = nz // 4
    for copy in copies[0]:
        copy.wait()
    layer(0, lambda f, rows8: below[f, rows8, :], inside(0, 1))
    for part in range(parts):
        if part < parts - 1:
            for copy in copies[part + 1]:
                copy.wait()
        lax.fori_loop(max(part * 4, 1), min(part * 4 + 4, nz - 1), body, 0)
        if part == parts - 1:
            layer(nz - 1, inside(nz - 1, -1), lambda f, rows8: above[f, rows8, :])
        send(part).start()
    for part in range(parts):
        send(part).wait()


def stencil(mag, vel, before, after, below, above):
    nz, nr, cells = mag.shape[1:]
    return pl.pallas_call(
        stencil_kernel,
        out_shape=pltpu.HBM(mag.shape, F32),
        in_specs=[HBM] * 2 + [VMEM] * 4,
        out_specs=HBM,
        scratch_shapes=[
            pltpu.VMEM((2, *mag.shape), F32),
            pltpu.VMEM(mag.shape, F32),
            pltpu.VMEM((4, nr // 8, 8, cells), F32),
            pltpu.SemaphoreType.DMA((2, nz // 4)),
            pltpu.SemaphoreType.DMA((nz // 4,)),
        ],
        compiler_params=params(16),
        cost_estimate=cost(40 << 20, 8 << 20),
        name="stencil",
    )(*pinned(mag, vel), before, after, below, above)


def decode_kernel(arrived, table, layers, vel, held, flux, out, parts, edge, wind, sems):
    nz, cells = flux.shape[1:]
    get_table = pltpu.make_async_copy(table, parts, sems.at[3])
    get_table.start()
    get_edge = pltpu.make_async_copy(held.at[1:3, :, 56:64, :], edge, sems.at[0])
    get_wind = pltpu.make_async_copy(vel.at[0, :, 56:64, :], wind, sems.at[1])
    get_edge.start()
    get_wind.start()
    high, low = split(jnp.transpose(arrived[...], (1, 0)))
    total = jnp.zeros((4 * nz, 2 * cells), F32)
    get_table.wait()
    for i in range(4):
        part = slice(i * 2 * nz, (i + 1) * 2 * nz)
        pair = jnp.concatenate([high[part], low[part]], 0)
        total = total + dot(pair, parts[i], NN)
    total = total[:, 0:cells] + total[:, cells : 2 * cells]
    total = (total[0 : 2 * nz] + total[2 * nz : 4 * nz]).reshape(2, nz, cells)
    flux[...] = total
    thickness = layers[...].astype(F32) * (1.0 / LW)
    by_radial = TIME_STEP / (2.0 * RADIAL_STEP)
    last = 1.0 - 0.5 * RADIAL_STEP
    fixed = TIME_STEP * DIFFUSIVITY / RADIAL_STEP**2 + DIFFUSIVITY * by_radial / last
    row = rows((nz, 8, cells))
    get_wind.wait()
    factor = jnp.where(row == 7, fixed - by_radial * wind[...], 0.0)
    get_edge.wait()
    for c in range(2):
        edge[c] = edge[c] - (thickness * total[c])[:, None, :] * factor
    put = pltpu.make_async_copy(edge, out.at[1:3, :, 56:64, :], sems.at[2])
    put.start()
    put.wait()


def decode(arrived, table, layers, vel, held):
    nz, nr, cells = held.shape[1:]
    return pl.pallas_call(
        decode_kernel,
        out_shape=(
            jax.ShapeDtypeStruct((2, nz, cells), F32),
            pltpu.HBM(held.shape, F32),
        ),
        in_specs=[VMEM, HBM, VMEM, HBM, HBM],
        out_specs=(VMEM, HBM),
        scratch_shapes=[
            pltpu.VMEM(table.shape, BF16),
            pltpu.VMEM((2, nz, 8, cells), F32),
            pltpu.VMEM((nz, 8, cells), F32),
            pltpu.SemaphoreType.DMA((4,)),
        ],
        input_output_aliases={4: 1},
        compiler_params=params(8),
        cost_estimate=cost(12 << 20, 1 << 20),
        name="decode",
    )(arrived, *pinned(table), layers.reshape(1, cells), *pinned(vel, held))


def neighbours(low, high, axis, periodic):
    count = lax.axis_size(axis)
    forward = [(i, i + 1) for i in range(count - 1)]
    if periodic:
        forward.append((count - 1, 0))
    backward = [(target, source) for source, target in forward]
    return lax.ppermute(high, axis, forward), lax.ppermute(low, axis, backward)


def shards(magnetic, velocity, wall_response, mode_slots, wall_layers):
    message, table = encode(magnetic, mode_slots)
    arrived = lax.all_to_all(message, BOTH, 0, 0, tiled=True)
    left, right, bottom, top = pack(magnetic, velocity)
    before, after = neighbours(left, right, "region", True)
    below, above = neighbours(bottom, top, "slab", False)
    replies = apply_wall(arrived, wall_response, before, after, below, above)
    returned = lax.all_to_all(replies, BOTH, 0, 0, tiled=True)
    stepped = stencil(magnetic, velocity, before, after, below, above)
    wall_flux, magnetic_next = decode(returned, table, wall_layers, velocity, stepped)
    return magnetic_next, wall_flux


def solution(mesh):
    placed = (
        P(None, "slab", None, "region"),
        P(None, "slab", None, "region"),
        P(BOTH, None, None),
        P(),
        P("region"),
    )
    return jax.shard_map(
        shards,
        mesh=mesh,
        in_specs=placed,
        out_specs=(P(None, "slab", None, "region"), P(None, "slab", "region")),
        check_vma=False,
    )
```

time: 81.1 us -> 71.3 us (0.88)
  the two profiles are of different devices: /device:TPU:71 before, /device:TPU:1 now
where the time goes in v2:
time: 71.3 us; the launch traced here: 71 us
  starting transfers between devices  43.3 us (61%)
  Pallas kernels  19 us (27%)
  waiting for transfers between devices  7.97 us (11%)
    all_to_all x1, starting transfers between devices, shards(): returned = lax.all_to_all(replies, BOTH, 0, 0, tiled=True)  18.4 us
    all_to_all x1, starting transfers between devices, shards(): arrived = lax.all_to_all(message, BOTH, 0, 0, tiled=True)  15.7 us
    all_to_all x1, waiting for transfers between devices, shards(): returned = lax.all_to_all(replies, BOTH, 0, 0, tiled=True)  6.5 us
    pallas_call x1, Pallas kernels, stencil(): pl.pallas_call(stencil_kernel, out_shape=pltpu.HBM(mag.shape, F32), in_sp...  6.4 us
    ppermute x2, starting transfers between devices, neighbours(): lax.ppermute(high, axis, forward)  4.94 us
    ppermute x2, starting transfers between devices, neighbours(): lax.ppermute(low, axis, backward)  4.32 us
    pallas_call x1, Pallas kernels, apply_wall(): pl.pallas_call(wall_kernel, out_shape=jax.ShapeDtypeStruct(arrived.shape,...  3.71 us
    pallas_call x1, Pallas kernels, pack(): pl.pallas_call(pack_kernel, out_shape=(edge, edge, pltpu.HBM((6, nr, cell...  3.32 us
  transfers between devices with their start and end apart: 6, of which 3 were waited for; matrix products, arithmetic and copies ran while one was open for 0% of the time, Pallas kernels for 14%

profile of v2, /device:TPU:1, one launch (start us, length us, event | category | flops | bytes accessed | tf_op | source)
XLA Modules:
  0.0 71.0 jit_solution(5326109143303236217)
XLA Ops:
  0.6 3.0 %encode.1 = (f32[256,128]{1,0:T(8,128)}, bf16[4,256,256]{2,1,0:T(8,128)(2,1)}) custom-call(f32[3,16,64,128]{3,2,1,0:T(8,128)} %mag.5, s32[8,128]{1,0:T(8,128)} %bitcast.13), custom_call_target="tpu_custom_call" | custom-call | flops 100663296 | bytes 1048576 | tf_op jit(solution)/shard_map/encode/pallas_call | solution.py:127
  3.7 15.7 %all-to-all-start = ((f32[256,1,128]{2,1,0:T(1,128)}), f32[256,1,128]{2,1,0:T(1,128)S(1)}, u32[]{:S(2)}, u32[]{:S(2)}) async-start(f32[256,1,128]{2,1,0:T(1,128)} %bitcast.2), calls=%async_computation | async-start | bytes 262144 | tf_op jit(solution)/shard_map/all_to_all | solution.py:439
  19.3 3.3 %pack.1 = (f32[6,8,128]{2,1,0:T(8,128)S(1)}, f32[6,8,128]{2,1,0:T(8,128)S(1)}, f32[6,64,128]{2,1,0:T(8,128)}, f32[6,64,128]{2,1,0:T(8,128)}) custom-call(f32[3,16,64,128]{3,2,1,0:T(8,128)} %mag.5, f32[3,16,64,128]{3,2,1,0:T(8,128)} %vel.5), custom_call_target="tpu_custom_call" | custom-call | flops 8388608 | bytes 4194304 | tf_op jit(solution)/shard_map/pack/pallas_call | solution.py:241
  22.7 3.5 %collective-permute-start.2 = (f32[6,64,128]{2,1,0:T(8,128)}, f32[6,64,128]{2,1,0:T(8,128)S(1)}, u32[]{:S(2)}, u32[]{:S(2)}) collective-permute-start(f32[6,64,128]{2,1,0:T(8,128)} %get-tuple-element.13), channel_id=1, source_target_pairs={{0,1},{1,2},{2,3},{3,4},{4,5},{5,6},{6,7},{7,8},{8,9},{9,10},{10,1... | collective-permute-start | bytes 589832 | tf_op jit(solution)/shard_map/ppermute | solution.py:434
  26.2 1.9 %collective-permute-start.3 = (f32[6,64,128]{2,1,0:T(8,128)}, f32[6,64,128]{2,1,0:T(8,128)S(1)}, u32[]{:S(2)}, u32[]{:S(2)}) collective-permute-start(f32[6,64,128]{2,1,0:T(8,128)} %get-tuple-element.14), channel_id=1, source_target_pairs={{1,0},{2,1},{3,2},{4,3},{5,4},{6,5},{7,6},{8,7},{9,8},{10,9},{11,1... | collective-permute-start | bytes 589832 | tf_op jit(solution)/shard_map/ppermute | solution.py:434
  28.1 1.4 %collective-permute-start = (f32[6,8,128]{2,1,0:T(8,128)S(1)}, f32[6,8,128]{2,1,0:T(8,128)S(1)}, u32[]{:S(2)}, u32[]{:S(2)}) collective-permute-start(f32[6,8,128]{2,1,0:T(8,128)S(1)} %get-tuple-element.11), channel_id=1, source_target_pairs={{0,32},{32,64},{64,96},{96,128},{128,160},{160,192},{192,224},{224... | collective-permute-start | bytes 73736 | tf_op jit(solution)/shard_map/ppermute | solution.py:434
  29.5 2.4 %collective-permute-start.1 = (f32[6,8,128]{2,1,0:T(8,128)S(1)}, f32[6,8,128]{2,1,0:T(8,128)S(1)}, u32[]{:S(2)}, u32[]{:S(2)}) collective-permute-start(f32[6,8,128]{2,1,0:T(8,128)S(1)} %get-tuple-element.12), channel_id=1, source_target_pairs={{32,0},{64,32},{96,64},{128,96},{160,128},{192,160},{224,192},{0,2... | collective-permute-start | bytes 73736 | tf_op jit(solution)/shard_map/ppermute | solution.py:434
  31.9 1.1 %collective-permute-done.rest_0_.before = f32[6,8,128]{2,1,0:T(8,128)S(1)} collective-permute-done((f32[6,8,128]{2,1,0:T(8,128)S(1)}, f32[6,8,128]{2,1,0:T(8,128)S(1)}, u32[]{:S(2)}, u32[]{:S(2)}) %collective-permute-start) | collective-permute-done | bytes 24608 | tf_op jit(solution)/shard_map/ppermute | solution.py:434
  33.1 0.0 collective-permute-done.1.rest_1_.after
  33.1 0.0 collective-permute-done.2.rest_2_.below
  33.1 0.3 collective-permute-done.3.rest_3_.above
  33.4 0.0 all-to-all-done
  33.4 3.7 %wall.2 = f32[256,128]{1,0:T(8,128)} custom-call(f32[256,128]{1,0:T(8,128)S(1)} %bitcast.10, f32[4,512,512]{2,1,0:T(8,128)} %wall.3, f32[6,8,128]{2,1,0:T(8,128)S(1)} %collective-permute-done.rest_0_.before, f32[6,8,128]{2,1,0:T(8,128)S(1)} %collective-permute-done.1.rest_1_.after, f32[6,64,128]{2,1,0:T(8,128)S(1)} %collective-permute-done.2.rest_2_.below, ...), custom_call_target="tpu_custom_call" | custom-call | flops 100663296 | bytes 4194304 | tf_op jit(solution)/shard_map/wall/pallas_call | solution.py:174
  37.1 18.4 %all-to-all-start.1 = ((f32[256,1,128]{2,1,0:T(1,128)}), f32[256,1,128]{2,1,0:T(1,128)S(1)}, u32[]{:S(2)}, u32[]{:S(2)}) async-start(f32[256,1,128]{2,1,0:T(1,128)} %bitcast.5), calls=%async_computation.1 | async-start | bytes 262144 | tf_op jit(solution)/shard_map/all_to_all | solution.py:444
  55.5 0.0 copy-start
  55.5 6.4 %stencil.1.held = f32[3,16,64,128]{3,2,1,0:T(8,128)} custom-call(f32[3,16,64,128]{3,2,1,0:T(8,128)} %mag.5, f32[3,16,64,128]{3,2,1,0:T(8,128)} %vel.5, f32[6,8,128]{2,1,0:T(8,128)S(1)} %collective-permute-done.rest_0_.before, f32[6,8,128]{2,1,0:T(8,128)S(1)} %collective-permute-done.1.rest_1_.after, f32[6,64,128]{2,1,0:T(8,128)S(1)} %collective-permute-done.2.rest_2_.below, ...), custom_call_target="tpu_custom_call" | custom-call | flops 41943040 | bytes 8388608 | tf_op jit(solution)/shard_map/stencil/pallas_call | solution.py:354
  61.9 6.5 %all-to-all-done.1 = f32[256,1,128]{2,1,0:T(1,128)S(1)} async-done(((f32[256,1,128]{2,1,0:T(1,128)}), f32[256,1,128]{2,1,0:T(1,128)S(1)}, u32[]{:S(2)}, u32[]{:S(2)}) %all-to-all-start.1) | async-done | bytes 131104 | tf_op jit(solution)/shard_map/all_to_all | solution.py:444
  68.4 0.0 copy-done
  68.4 2.6 %decode.1 = (f32[2,16,128]{2,1,0:T(8,128)}, f32[3,16,64,128]{3,2,1,0:T(8,128)}) custom-call(f32[256,128]{1,0:T(8,128)S(1)} %bitcast.11, bf16[4,256,256]{2,1,0:T(8,128)(2,1)} %get-tuple-element.15.table, s32[1,128]{1,0:T(1,128)S(1)} %bitcast.12, f32[3,16,64,128]{3,2,1,0:T(8,128)} %vel.5, f32[3,16,64,128]{3,2,1,0:T(8,128)} %stencil.1.held), custom_call_target="tpu_custom_call", output_to_operand_aliasing={{1}: (4, {})} | custom-call | flops 12582912 | bytes 1048576 | tf_op jit(solution)/shard_map/decode/pallas_call | solution.py:407
Async XLA Ops:
  3.7 29.7 %all-to-all-start = ((f32[256,1,128]{2,1,0:T(1,128)}), f32[256,1,128]{2,1,0:T(1,128)S(1)}, u32[]{:S(2)}, u32[]{:S(2)}) async-start(f32[256,1,128]{2,1,0:T(1,128)} %bitcast.2), calls=%async_computation | async-start | bytes 262144 | tf_op jit(solution)/shard_map/all_to_all | solution.py:439
  22.7 10.4 %collective-permute-start.2 = (f32[6,64,128]{2,1,0:T(8,128)}, f32[6,64,128]{2,1,0:T(8,128)S(1)}, u32[]{:S(2)}, u32[]{:S(2)}) collective-permute-start(f32[6,64,128]{2,1,0:T(8,128)} %get-tuple-element.13), channel_id=1, source_target_pairs={{0,1},{1,2},{2,3},{3,4},{4,5},{5,6},{6,7},{7,8},{8,9},{9,10},{10,1... | collective-permute-start | bytes 589832 | tf_op jit(solution)/shard_map/ppermute | solution.py:434
  26.2 7.2 %collective-permute-start.3 = (f32[6,64,128]{2,1,0:T(8,128)}, f32[6,64,128]{2,1,0:T(8,128)S(1)}, u32[]{:S(2)}, u32[]{:S(2)}) collective-permute-start(f32[6,64,128]{2,1,0:T(8,128)} %get-tuple-element.14), channel_id=1, source_target_pairs={{1,0},{2,1},{3,2},{4,3},{5,4},{6,5},{7,6},{8,7},{9,8},{10,9},{11,1... | collective-permute-start | bytes 589832 | tf_op jit(solution)/shard_map/ppermute | solution.py:434
  28.1 4.9 %collective-permute-start = (f32[6,8,128]{2,1,0:T(8,128)S(1)}, f32[6,8,128]{2,1,0:T(8,128)S(1)}, u32[]{:S(2)}, u32[]{:S(2)}) collective-permute-start(f32[6,8,128]{2,1,0:T(8,128)S(1)} %get-tuple-element.11), channel_id=1, source_target_pairs={{0,32},{32,64},{64,96},{96,128},{128,160},{160,192},{192,224},{224... | collective-permute-start | bytes 73736 | tf_op jit(solution)/shard_map/ppermute | solution.py:434
  29.5 3.5 %collective-permute-start.1 = (f32[6,8,128]{2,1,0:T(8,128)S(1)}, f32[6,8,128]{2,1,0:T(8,128)S(1)}, u32[]{:S(2)}, u32[]{:S(2)}) collective-permute-start(f32[6,8,128]{2,1,0:T(8,128)S(1)} %get-tuple-element.12), channel_id=1, source_target_pairs={{32,0},{64,32},{96,64},{128,96},{160,128},{192,160},{224,192},{0,2... | collective-permute-start | bytes 73736 | tf_op jit(solution)/shard_map/ppermute | solution.py:434
  37.1 31.3 %all-to-all-start.1 = ((f32[256,1,128]{2,1,0:T(1,128)}), f32[256,1,128]{2,1,0:T(1,128)S(1)}, u32[]{:S(2)}, u32[]{:S(2)}) async-start(f32[256,1,128]{2,1,0:T(1,128)} %bitcast.5), calls=%async_computation.1 | async-start | bytes 262144 | tf_op jit(solution)/shard_map/all_to_all | solution.py:444
  55.5 12.9 %copy-start = (s32[128]{0:T(128)S(1)}, s32[128]{0:T(128)}, u32[]{:S(2)}) copy-start(s32[128]{0:T(128)} %param.9) | copy-start | bytes 1540

commit v3 on v2

--- a/solution.py
+++ b/solution.py
@@ -25,6 +25,10 @@
 
 def pinned(*arrays):
     return [pltpu.with_memory_space_constraint(a, pltpu.HBM) for a in arrays]
+
+
+def resident(*arrays):
+    return [pltpu.with_memory_space_constraint(a, pltpu.VMEM) for a in arrays]
 
 
 def params(mib):
@@ -77,13 +81,22 @@
     return x
 
 
-def encode_kernel(mag, modes, message, table, edge, slots, turned, parts, sems):
+def encode_kernel(mag, vel, modes, message, parts, ends_a, ends_b, edge, slots, turned, sems, end_sems):
     count, cells = parts.shape[1], edge.shape[3]
     nmodes = 4 * count
     get_modes = pltpu.make_async_copy(modes, slots, sems.at[0])
     get_edge = pltpu.make_async_copy(mag.at[1:3, :, 56:64, :], edge, sems.at[1])
     get_modes.start()
     get_edge.start()
+    odd = lax.axis_index("slab") % 2
+    last = mag.shape[1] - 1
+    ends = []
+    for k, ref in enumerate((mag, vel)):
+        for n, (target, layer) in enumerate(((ends_a, last * (1 - odd)), (ends_b, last * odd))):
+            ends.append(
+                pltpu.make_async_copy(ref.at[:, layer], target.at[pl.ds(3 * k, 3)], end_sems.at[k, n])
+            )
+            ends[-1].start()
     first = lax.axis_index("region") * cells
     odd_cell = (2 * (first + lanes((cells, cells))) + 1).astype(F32)
     get_modes.wait()
@@ -101,8 +114,6 @@
             part = slice(half * 128, half * 128 + 128)
             parts[i, part, 0:cells] = high
             parts[i, part, cells : 2 * cells] = low
-    put_table = pltpu.make_async_copy(parts, table, sems.at[2])
-    put_table.start()
     get_edge.wait()
     trace = edge[:, :, 7, :].reshape(32, cells)
     high, low = split(jnp.concatenate([trace] * 4, 0))
@@ -118,36 +129,41 @@
         both = (both[:, 0:128] + both[:, 128:256]) * jnp.concatenate(scale, 0)
         out = jnp.where(lane == i, both, out)
     message[...] = out
-    put_table.wait()
-
-
-def encode(mag, modes):
-    nz, _, cells = mag.shape[1:]
+    for copy in ends:
+        copy.wait()
+
+
+def encode(mag, vel, modes):
+    nz, nr, cells = mag.shape[1:]
     count = modes.size // 4
+    layer = pltpu.VMEM((6, nr, cells), F32)
     return pl.pallas_call(
         encode_kernel,
         out_shape=(
             jax.ShapeDtypeStruct((count, 128), F32),
-            pltpu.HBM((4, count, 2 * cells), BF16),
+            pltpu.VMEM((4, count, 2 * cells), BF16),
+            layer,
+            layer,
         ),
-        in_specs=[HBM, HBM],
-        out_specs=(VMEM, HBM),
+        in_specs=[HBM, HBM, HBM],
+        out_specs=(VMEM,) * 4,
         scratch_shapes=[
             pltpu.VMEM((2, nz, 8, cells), F32),
             pltpu.VMEM((8, 128), jnp.int32),
             pltpu.VMEM((128, 128), F32),
-            pltpu.VMEM((4, count, 2 * cells), BF16),
-            pltpu.SemaphoreType.DMA((3,)),
+            pltpu.SemaphoreType.DMA((2,)),
+            pltpu.SemaphoreType.DMA((2, 2)),
         ],
         compiler_params=params(8),
         cost_estimate=cost(3 * 2 * 1024 * 128 * 128, 1 << 20),
         name="encode",
-    )(*pinned(mag, modes.reshape(8, 128)))
-
-
-def wall_kernel(arrived, wall, *rest):
+    )(*pinned(mag, vel, modes.reshape(8, 128)))
+
+
+def wall_kernel(arrived, near, wall, *rest):
     message, held, sems = rest[-3:]
-    copies = [pltpu.make_async_copy(wall.at[i], held.at[i], sems.at[i]) for i in range(4)]
+    count = near.shape[0]
+    copies = [pltpu.make_async_copy(wall.at[count + i], held.at[i], sems.at[i]) for i in range(held.shape[0])]
     for copy in copies:
         copy.start()
     x = arrived[0:32, :]
@@ -159,8 +175,11 @@
     response = jnp.zeros(coeff.shape, F32)
     owner = rows(coeff.shape) >> 1
     for i in range(4):
-        copies[i].wait()
-        high, low = split(held[i])
+        if i < count:
+            high, low = split(near[i])
+        else:
+            copies[i - count].wait()
+            high, low = split(held[i - count])
         a = dot(stacked, high, NT)
         b = dot(stacked, low, NT)
         response = jnp.where(owner == i, a[0:8] + (a[8:16] + b[0:8]), response)
@@ -170,17 +189,20 @@
         message[r * 32 : (r + 1) * 32, :] = y
 
 
-def apply_wall(arrived, wall, *earlier):
+def apply_wall(arrived, near, wall, *earlier):
     return pl.pallas_call(
         wall_kernel,
         out_shape=jax.ShapeDtypeStruct(arrived.shape, F32),
-        in_specs=[VMEM, HBM] + [ANY] * len(earlier),
+        in_specs=[VMEM, VMEM, HBM] + [ANY] * len(earlier),
         out_specs=VMEM,
-        scratch_shapes=[pltpu.VMEM(wall.shape, F32), pltpu.SemaphoreType.DMA((4,))],
+        scratch_shapes=[
+            pltpu.VMEM((wall.shape[0] - near.shape[0], *wall.shape[1:]), F32),
+            pltpu.SemaphoreType.DMA((wall.shape[0] - near.shape[0],)),
+        ],
         compiler_params=params(16),
         cost_estimate=cost(3 * 2 * 16 * 512 * 512 * 4, 4 << 20),
         name="wall",
-    )(arrived, *pinned(wall), *earlier)
+    )(arrived, *resident(near), *pinned(wall), *earlier)
 
 
 def fetch(mag, vel, held, sems):
@@ -195,13 +217,15 @@
     ]
 
 
-def pack_kernel(mag, vel, left, right, bottom, top, held, low_sems, high_sems, sems):
+def pack_kernel(mag, vel, wall, ends_a, ends_b, near_wall, held, sems, wall_sem):
     nz, nr, cells = mag.shape[1:]
     lane = lanes((8, cells))
     copies = fetch(mag, vel, held, sems)
     for pair in copies:
         for copy in pair:
             copy.start()
+    get_wall = pltpu.make_async_copy(wall.at[pl.ds(0, near_wall.shape[0])], near_wall, wall_sem)
+    get_wall.start()
 
     def body(z, carry):
         low, high = list(carry[0]), list(carry[1])
@@ -216,46 +240,38 @@
 
     zero = (jnp.zeros((8, cells), F32),) * 6
     carry = (zero, zero)
-    ends = []
     for part, pair in enumerate(copies):
         for copy in pair:
             copy.wait()
-        for k in range(2):
-            if part == 0:
-                ends.append(pltpu.make_async_copy(held.at[k, :, 0], bottom.at[pl.ds(3 * k, 3)], low_sems.at[k]))
-                ends[-1].start()
-            if part == nz // 4 - 1:
-                ends.append(pltpu.make_async_copy(held.at[k, :, nz - 1], top.at[pl.ds(3 * k, 3)], high_sems.at[k]))
-                ends[-1].start()
         carry = lax.fori_loop(part * 4, part * 4 + 4, body, carry)
+    even = lax.axis_index("region") % 2 == 0
     for f in range(6):
-        left[f] = carry[0][f]
-        right[f] = carry[1][f]
-    for copy in ends:
-        copy.wait()
-
-
-def pack(mag, vel):
+        low, high = carry[0][f], carry[1][f]
+        ends_a[f] = jnp.where(even, high, low)
+        ends_b[f] = jnp.where(even, low, high)
+    get_wall.wait()
+
+
+def pack(mag, vel, wall):
     nz, nr, cells = mag.shape[1:]
-    edge = jax.ShapeDtypeStruct((6, 8, cells), F32)
+    edge = pltpu.VMEM((6, 8, cells), F32)
     return pl.pallas_call(
         pack_kernel,
-        out_shape=(edge, edge, pltpu.HBM((6, nr, cells), F32), pltpu.HBM((6, nr, cells), F32)),
-        in_specs=[HBM, HBM],
-        out_specs=(VMEM, VMEM, HBM, HBM),
+        out_shape=(edge, edge, pltpu.VMEM((2, *wall.shape[1:]), F32)),
+        in_specs=[HBM, HBM, HBM],
+        out_specs=(VMEM, VMEM, VMEM),
         scratch_shapes=[
             pltpu.VMEM((2, *mag.shape), F32),
-            pltpu.SemaphoreType.DMA((2,)),
-            pltpu.SemaphoreType.DMA((2,)),
             pltpu.SemaphoreType.DMA((2, nz // 4)),
+            pltpu.SemaphoreType.DMA,
         ],
         compiler_params=params(12),
         cost_estimate=cost(8 << 20, 4 << 20),
         name="pack",
-    )(*pinned(mag, vel))
-
-
-def stencil_kernel(mag, vel, before, after, below, above, out, held, stepped, factors, gets, sems):
+    )(*pinned(mag, vel, wall))
+
+
+def stencil_kernel(mag, vel, side_a, side_b, end_a, end_b, out, edge, held, stepped, factors, sides, gets, sems):
     nz, nr, cells = mag.shape[1:]
     lane = lanes((8, cells))
     row = rows((8, cells))
@@ -263,6 +279,10 @@
     for pair in copies:
         for copy in pair:
             copy.start()
+    even = lax.axis_index("region") % 2 == 0
+    sides[0] = jnp.where(even, side_b[...], side_a[...])
+    sides[1] = jnp.where(even, side_a[...], side_b[...])
+    even_slab = lax.axis_index("slab") % 2 == 0
     angle_step = 2.0 * math.pi / (cells * 8)
     spread = TIME_STEP * DIFFUSIVITY
     by_radial = TIME_STEP / (2.0 * RADIAL_STEP)
@@ -294,8 +314,8 @@
                     outer = jnp.where(row == 7, here, pltpu.roll(here, 7, 0))
                 else:
                     outer = ref[c, z, t * 8 + 1 : t * 8 + 9, :]
-                far = pltpu.roll(after[f], (255 - j) & 127, 1)
-                near = pltpu.roll(before[f], (129 - j) & 127, 1)
+                far = pltpu.roll(sides[1, f], (255 - j) & 127, 1)
+                near = pltpu.roll(sides[0, f], (129 - j) & 127, 1)
                 p_next = jnp.where(lane == cells - 1, far, pltpu.roll(here, cells - 1, 1))
                 p_prev = jnp.where(lane == 0, near, pltpu.roll(here, 1, 1))
                 z_next = up(f, rows8)
@@ -320,6 +340,11 @@
                 value = value + (ur * dr[c] - up_ * dp[c]) - uz * dz[c]
                 value = value + (br * dr[c + 3] + bp * dp[c + 3]) + bz * dz[c + 3]
                 stepped[c, z, rows8, :] = value
+                if c and t == nr // 8 - 1:
+                    edge[c - 1, z] = value
+            if t == nr // 8 - 1:
+                at_wall = second_radial + spread / (2.0 * RADIAL_STEP) / (1.0 - 0.5 * RADIAL_STEP)
+                edge[2, z] = jnp.where(row == 7, at_wall - by_radial * x[3], 0.0)
 
     def inside(z, step):
         return lambda f, rows8: held[f // 3, f % 3, z + step, rows8, :]
@@ -336,73 +361,61 @@
     parts = nz // 4
     for copy in copies[0]:
         copy.wait()
-    layer(0, lambda f, rows8: below[f, rows8, :], inside(0, 1))
+    layer(0, lambda f, rows8: jnp.where(even_slab, end_b[f, rows8, :], end_a[f, rows8, :]), inside(0, 1))
     for part in range(parts):
         if part < parts - 1:
             for copy in copies[part + 1]:
                 copy.wait()
         lax.fori_loop(max(part * 4, 1), min(part * 4 + 4, nz - 1), body, 0)
         if part == parts - 1:
-            layer(nz - 1, inside(nz - 1, -1), lambda f, rows8: above[f, rows8, :])
+            layer(nz - 1, inside(nz - 1, -1), lambda f, rows8: jnp.where(even_slab, end_a[f, rows8, :], end_b[f, rows8, :]))
         send(part).start()
     for part in range(parts):
         send(part).wait()
 
 
-def stencil(mag, vel, before, after, below, above):
+def stencil(mag, vel, *halos):
     nz, nr, cells = mag.shape[1:]
     return pl.pallas_call(
         stencil_kernel,
-        out_shape=pltpu.HBM(mag.shape, F32),
+        out_shape=(pltpu.HBM(mag.shape, F32), pltpu.VMEM((3, nz, 8, cells), F32)),
         in_specs=[HBM] * 2 + [VMEM] * 4,
-        out_specs=HBM,
+        out_specs=(HBM, VMEM),
         scratch_shapes=[
             pltpu.VMEM((2, *mag.shape), F32),
             pltpu.VMEM(mag.shape, F32),
             pltpu.VMEM((4, nr // 8, 8, cells), F32),
+            pltpu.VMEM((2, 6, 8, cells), F32),
             pltpu.SemaphoreType.DMA((2, nz // 4)),
             pltpu.SemaphoreType.DMA((nz // 4,)),
         ],
         compiler_params=params(16),
         cost_estimate=cost(40 << 20, 8 << 20),
         name="stencil",
-    )(*pinned(mag, vel), before, after, below, above)
-
-
-def decode_kernel(arrived, table, layers, vel, held, flux, out, parts, edge, wind, sems):
+    )(*pinned(mag, vel), *halos)
+
+
+def decode_kernel(arrived, table, layers, edge, held, flux, out, fixed, sem):
+    del held
     nz, cells = flux.shape[1:]
-    get_table = pltpu.make_async_copy(table, parts, sems.at[3])
-    get_table.start()
-    get_edge = pltpu.make_async_copy(held.at[1:3, :, 56:64, :], edge, sems.at[0])
-    get_wind = pltpu.make_async_copy(vel.at[0, :, 56:64, :], wind, sems.at[1])
-    get_edge.start()
-    get_wind.start()
     high, low = split(jnp.transpose(arrived[...], (1, 0)))
     total = jnp.zeros((4 * nz, 2 * cells), F32)
-    get_table.wait()
     for i in range(4):
         part = slice(i * 2 * nz, (i + 1) * 2 * nz)
         pair = jnp.concatenate([high[part], low[part]], 0)
-        total = total + dot(pair, parts[i], NN)
+        total = total + dot(pair, table[i], NN)
     total = total[:, 0:cells] + total[:, cells : 2 * cells]
     total = (total[0 : 2 * nz] + total[2 * nz : 4 * nz]).reshape(2, nz, cells)
+    thickness = layers[...].astype(F32) * (1.0 / LW)
+    for c in range(2):
+        fixed[c] = edge[c] - (thickness * total[c])[:, None, :] * edge[2]
+    put = pltpu.make_async_copy(fixed, out.at[1:3, :, 56:64, :], sem)
+    put.start()
     flux[...] = total
-    thickness = layers[...].astype(F32) * (1.0 / LW)
-    by_radial = TIME_STEP / (2.0 * RADIAL_STEP)
-    last = 1.0 - 0.5 * RADIAL_STEP
-    fixed = TIME_STEP * DIFFUSIVITY / RADIAL_STEP**2 + DIFFUSIVITY * by_radial / last
-    row = rows((nz, 8, cells))
-    get_wind.wait()
-    factor = jnp.where(row == 7, fixed - by_radial * wind[...], 0.0)
-    get_edge.wait()
-    for c in range(2):
-        edge[c] = edge[c] - (thickness * total[c])[:, None, :] * factor
-    put = pltpu.make_async_copy(edge, out.at[1:3, :, 56:64, :], sems.at[2])
-    put.start()
     put.wait()
 
 
-def decode(arrived, table, layers, vel, held):
+def decode(arrived, table, layers, edge, held):
     nz, nr, cells = held.shape[1:]
     return pl.pallas_call(
         decode_kernel,
@@ -410,40 +423,38 @@
             jax.ShapeDtypeStruct((2, nz, cells), F32),
             pltpu.HBM(held.shape, F32),
         ),
-        in_specs=[VMEM, HBM, VMEM, HBM, HBM],
+        in_specs=[VMEM, VMEM, VMEM, VMEM, HBM],
         out_specs=(VMEM, HBM),
-        scratch_shapes=[
-            pltpu.VMEM(table.shape, BF16),
-            pltpu.VMEM((2, nz, 8, cells), F32),
-            pltpu.VMEM((nz, 8, cells), F32),
-            pltpu.SemaphoreType.DMA((4,)),
-        ],
+        scratch_shapes=[pltpu.VMEM((2, nz, 8, cells), F32), pltpu.SemaphoreType.DMA],
         input_output_aliases={4: 1},
         compiler_params=params(8),
         cost_estimate=cost(12 << 20, 1 << 20),
         name="decode",
-    )(arrived, *pinned(table), layers.reshape(1, cells), *pinned(vel, held))
-
-
-def neighbours(low, high, axis, periodic):
+    )(arrived, *resident(table), layers.reshape(1, cells), *resident(edge), *pinned(held))
+
+
+def swap(payload, axis, offset, periodic):
     count = lax.axis_size(axis)
-    forward = [(i, i + 1) for i in range(count - 1)]
-    if periodic:
-        forward.append((count - 1, 0))
-    backward = [(target, source) for source, target in forward]
-    return lax.ppermute(high, axis, forward), lax.ppermute(low, axis, backward)
+    pairs = []
+    for i in range(offset, count - 1 + offset, 2):
+        j = i + 1
+        if j < count or periodic:
+            pairs += [(i, j % count), (j % count, i)]
+    return lax.ppermute(payload, axis, pairs)
 
 
 def shards(magnetic, velocity, wall_response, mode_slots, wall_layers):
-    message, table = encode(magnetic, mode_slots)
+    message, table, ends_a, ends_b = encode(magnetic, velocity, mode_slots)
     arrived = lax.all_to_all(message, BOTH, 0, 0, tiled=True)
-    left, right, bottom, top = pack(magnetic, velocity)
-    before, after = neighbours(left, right, "region", True)
-    below, above = neighbours(bottom, top, "slab", False)
-    replies = apply_wall(arrived, wall_response, before, after, below, above)
+    end_b = swap(ends_b, "slab", 1, False)
+    sides_a, sides_b, near = pack(magnetic, velocity, wall_response)
+    side_b = swap(sides_b, "region", 1, True)
+    side_a = swap(sides_a, "region", 0, True)
+    end_a = swap(ends_a, "slab", 0, False)
+    replies = apply_wall(arrived, near, wall_response, side_a, side_b, end_a, end_b)
     returned = lax.all_to_all(replies, BOTH, 0, 0, tiled=True)
-    stepped = stencil(magnetic, velocity, before, after, below, above)
-    wall_flux, magnetic_next = decode(returned, table, wall_layers, velocity, stepped)
+    stepped, edge = stencil(magnetic, velocity, side_a, side_b, end_a, end_b)
+    wall_flux, magnetic_next = decode(returned, table, wall_layers, edge, stepped)
     return magnetic_next, wall_flux
 
 

time: 71.3 us -> 62.5 us (0.88)
  starting transfers between devices: 43.3 us -> 36 us
  Pallas kernels: 19 us -> 16.6 us
  waiting for transfers between devices: 7.97 us -> 8.94 us
    all_to_all x1, starting transfers between devices: 18.4 us -> 12.8 us  [shards(): returned = lax.all_to_all(replies, BOTH, 0, 0, tiled=True)]
    ppermute x4, starting transfers between devices: 9.26 us -> 7.58 us  [swap(): return lax.ppermute(payload, axis, pairs)]
    pallas_call x1, Pallas kernels: 2.59 us -> 1.56 us  [decode(): pl.pallas_call(decode_kernel, out_shape=(jax.ShapeDtypeStruct((2, nz, cel...]
    ppermute x4, waiting for transfers between devices: 1.47 us -> 2.39 us  [swap(): return lax.ppermute(payload, axis, pairs)]
    pallas_call x1, Pallas kernels: 3.71 us -> 2.91 us  [apply_wall(): pl.pallas_call(wall_kernel, out_shape=jax.ShapeDtypeStruct(arrived.shape,...]
  transfers between devices with their start and end apart: 6 -> 6, of which waited for: 3 -> 2; matrix products, arithmetic and copies ran while one was open for 0% -> 0% of each run, Pallas kernels for 14% -> 15%
where the time goes in v3:
time: 62.5 us; the launch traced here: 62.3 us
  starting transfers between devices  36 us (58%)
  Pallas kernels  16.6 us (27%)
  waiting for transfers between devices  8.94 us (14%)
  between operations  0.7 us (1%)
    all_to_all x1, starting transfers between devices, shards(): arrived = lax.all_to_all(message, BOTH, 0, 0, tiled=True)  15.7 us
    all_to_all x1, starting transfers between devices, shards(): returned = lax.all_to_all(replies, BOTH, 0, 0, tiled=True)  12.8 us
    ppermute x4, starting transfers between devices, swap(): return lax.ppermute(payload, axis, pairs)  7.58 us
    all_to_all x1, waiting for transfers between devices, shards(): returned = lax.all_to_all(replies, BOTH, 0, 0, tiled=True)  6.55 us
    pallas_call x1, Pallas kernels, stencil(): pl.pallas_call(stencil_kernel, out_shape=(pltpu.HBM(mag.shape, F32), pltp...  6.37 us
    pallas_call x1, Pallas kernels, pack(): pl.pallas_call(pack_kernel, out_shape=(edge, edge, pltpu.VMEM((2, *wall.s...  3.11 us
    pallas_call x1, Pallas kernels, apply_wall(): pl.pallas_call(wall_kernel, out_shape=jax.ShapeDtypeStruct(arrived.shape,...  2.91 us
    pallas_call x1, Pallas kernels, encode(): pl.pallas_call(encode_kernel, out_shape=(jax.ShapeDtypeStruct((count, 128...  2.67 us
  transfers between devices with their start and end apart: 6, of which 2 were waited for; matrix products, arithmetic and copies ran while one was open for 0% of the time, Pallas kernels for 15%

profile of v3, /device:TPU:1, one launch (start us, length us, event | category | flops | bytes accessed | tf_op | source)
XLA Modules:
  0.0 62.3 jit_solution(9256683783815013195)
XLA Ops:
  0.6 2.7 %encode.1 = (f32[256,128]{1,0:T(8,128)}, bf16[4,256,256]{2,1,0:T(8,128)(2,1)S(1)}, f32[6,64,128]{2,1,0:T(8,128)}, f32[6,64,128]{2,1,0:T(8,128)S(1)}) custom-call(f32[3,16,64,128]{3,2,1,0:T(8,128)} %mag.5, f32[3,16,64,128]{3,2,1,0:T(8,128)} %vel.5, s32[8,128]{1,0:T(8,128)} %bitcast.13), custom_call_target="tpu_custom_call" | custom-call | flops 100663296 | bytes 1048576 | tf_op jit(solution)/shard_map/encode/pallas_call | solution.py:140
  3.3 15.7 %all-to-all-start = ((f32[256,1,128]{2,1,0:T(1,128)}), f32[256,1,128]{2,1,0:T(1,128)S(1)}, u32[]{:S(2)}, u32[]{:S(2)}) async-start(f32[256,1,128]{2,1,0:T(1,128)} %bitcast.2), calls=%async_computation | async-start | bytes 262144 | tf_op jit(solution)/shard_map/all_to_all | solution.py:448
  19.0 2.2 %collective-permute-start.2 = (f32[6,64,128]{2,1,0:T(8,128)}, f32[6,64,128]{2,1,0:T(8,128)S(1)}, u32[]{:S(2)}, u32[]{:S(2)}) collective-permute-start(f32[6,64,128]{2,1,0:T(8,128)} %get-tuple-element.17), channel_id=1, source_target_pairs={{0,1},{1,0},{2,3},{3,2},{4,5},{5,4},{6,7},{7,6},{8,9},{9,8},{10,11... | collective-permute-start | bytes 589832 | tf_op jit(solution)/shard_map/ppermute | solution.py:443
  21.2 1.9 %collective-permute-start.3 = (f32[6,64,128]{2,1,0:T(8,128)S(1)}, f32[6,64,128]{2,1,0:T(8,128)S(1)}, u32[]{:S(2)}, u32[]{:S(2)}) collective-permute-start(f32[6,64,128]{2,1,0:T(8,128)S(1)} %get-tuple-element.18), channel_id=1, source_target_pairs={{1,2},{2,1},{3,4},{4,3},{5,6},{6,5},{7,8},{8,7},{9,10},{10,9},{11,... | collective-permute-start | bytes 589832 | tf_op jit(solution)/shard_map/ppermute | solution.py:443
  23.1 3.1 %pack.1 = (f32[6,8,128]{2,1,0:T(8,128)S(1)}, f32[6,8,128]{2,1,0:T(8,128)S(1)}, f32[2,512,512]{2,1,0:T(8,128)S(1)}) custom-call(f32[3,16,64,128]{3,2,1,0:T(8,128)} %mag.5, f32[3,16,64,128]{3,2,1,0:T(8,128)} %vel.5, f32[4,512,512]{2,1,0:T(8,128)} %wall.5), custom_call_target="tpu_custom_call" | custom-call | flops 8388608 | bytes 4194304 | tf_op jit(solution)/shard_map/pack/pallas_call | solution.py:258
  26.3 1.0 %collective-permute-start = (f32[6,8,128]{2,1,0:T(8,128)S(1)}, f32[6,8,128]{2,1,0:T(8,128)S(1)}, u32[]{:S(2)}, u32[]{:S(2)}) collective-permute-start(f32[6,8,128]{2,1,0:T(8,128)S(1)} %get-tuple-element.15), channel_id=1, source_target_pairs={{0,32},{32,0},{64,96},{96,64},{128,160},{160,128},{192,224},{224,1... | collective-permute-start | bytes 73736 | tf_op jit(solution)/shard_map/ppermute | solution.py:443
  27.3 2.4 %collective-permute-start.1 = (f32[6,8,128]{2,1,0:T(8,128)S(1)}, f32[6,8,128]{2,1,0:T(8,128)S(1)}, u32[]{:S(2)}, u32[]{:S(2)}) collective-permute-start(f32[6,8,128]{2,1,0:T(8,128)S(1)} %get-tuple-element.16), channel_id=1, source_target_pairs={{32,64},{64,32},{96,128},{128,96},{160,192},{192,160},{224,0},{0,2... | collective-permute-start | bytes 73736 | tf_op jit(solution)/shard_map/ppermute | solution.py:443
  29.7 0.0 collective-permute-done.rest_0_.side_a
  29.7 2.4 %collective-permute-done.1.rest_1_.side_b = f32[6,8,128]{2,1,0:T(8,128)S(1)} collective-permute-done((f32[6,8,128]{2,1,0:T(8,128)S(1)}, f32[6,8,128]{2,1,0:T(8,128)S(1)}, u32[]{:S(2)}, u32[]{:S(2)}) %collective-permute-start.1) | collective-permute-done | bytes 24608 | tf_op jit(solution)/shard_map/ppermute | solution.py:443
  32.1 0.0 collective-permute-done.2.rest_2_.end_a
  32.1 0.0 collective-permute-done.3.rest_3_.end_b
  32.1 0.0 all-to-all-done
  32.1 2.9 %wall.4 = f32[256,128]{1,0:T(8,128)} custom-call(f32[256,128]{1,0:T(8,128)S(1)} %bitcast.10, f32[2,512,512]{2,1,0:T(8,128)S(1)} %get-tuple-element.14.near, f32[4,512,512]{2,1,0:T(8,128)} %wall.5, f32[6,8,128]{2,1,0:T(8,128)S(1)} %collective-permute-done.rest_0_.side_a, f32[6,8,128]{2,1,0:T(8,128)S(1)} %collective-permute-done.1.rest_1_.side_b, ...), custom_call_target="tpu_custom_call" | custom-call | flops 100663296 | bytes 4194304 | tf_op jit(solution)/shard_map/wall/pallas_call | solution.py:193
  35.0 12.8 %all-to-all-start.1 = ((f32[256,1,128]{2,1,0:T(1,128)}), f32[256,1,128]{2,1,0:T(1,128)S(1)}, u32[]{:S(2)}, u32[]{:S(2)}) async-start(f32[256,1,128]{2,1,0:T(1,128)} %bitcast.5), calls=%async_computation.1 | async-start | bytes 262144 | tf_op jit(solution)/shard_map/all_to_all | solution.py:455
  47.8 0.0 copy-start
  47.8 6.4 %stencil.1 = (f32[3,16,64,128]{3,2,1,0:T(8,128)}, f32[3,16,8,128]{3,2,1,0:T(8,128)S(1)}) custom-call(f32[3,16,64,128]{3,2,1,0:T(8,128)} %mag.5, f32[3,16,64,128]{3,2,1,0:T(8,128)} %vel.5, f32[6,8,128]{2,1,0:T(8,128)S(1)} %collective-permute-done.rest_0_.side_a, f32[6,8,128]{2,1,0:T(8,128)S(1)} %collective-permute-done.1.rest_1_.side_b, ...), custom_call_target="tpu_custom_call" | custom-call | flops 41943040 | bytes 8388608 | tf_op jit(solution)/shard_map/stencil/pallas_call | solution.py:379
  54.2 6.5 %all-to-all-done.1 = f32[256,1,128]{2,1,0:T(1,128)S(1)} async-done(((f32[256,1,128]{2,1,0:T(1,128)}), f32[256,1,128]{2,1,0:T(1,128)S(1)}, u32[]{:S(2)}, u32[]{:S(2)}) %all-to-all-start.1) | async-done | bytes 131104 | tf_op jit(solution)/shard_map/all_to_all | solution.py:455
  60.8 0.0 copy-done
  60.8 1.6 %decode.1 = (f32[2,16,128]{2,1,0:T(8,128)}, f32[3,16,64,128]{3,2,1,0:T(8,128)}) custom-call(f32[256,128]{1,0:T(8,128)S(1)} %bitcast.11, bf16[4,256,256]{2,1,0:T(8,128)(2,1)S(1)} %get-tuple-element.19.table, s32[1,128]{1,0:T(1,128)S(1)} %bitcast.12, f32[3,16,8,128]{3,2,1,0:T(8,128)S(1)} %get-tuple-element.20.edge, ...), custom_call_target="tpu_custom_call", output_to_operand_aliasing={{1}: (4, {})} | custom-call | flops 12582912 | bytes 1048576 | tf_op jit(solution)/shard_map/decode/pallas_call | solution.py:420
Async XLA Ops:
  3.3 28.8 %all-to-all-start = ((f32[256,1,128]{2,1,0:T(1,128)}), f32[256,1,128]{2,1,0:T(1,128)S(1)}, u32[]{:S(2)}, u32[]{:S(2)}) async-start(f32[256,1,128]{2,1,0:T(1,128)} %bitcast.2), calls=%async_computation | async-start | bytes 262144 | tf_op jit(solution)/shard_map/all_to_all | solution.py:448
  19.0 13.1 %collective-permute-start.2 = (f32[6,64,128]{2,1,0:T(8,128)}, f32[6,64,128]{2,1,0:T(8,128)S(1)}, u32[]{:S(2)}, u32[]{:S(2)}) collective-permute-start(f32[6,64,128]{2,1,0:T(8,128)} %get-tuple-element.17), channel_id=1, source_target_pairs={{0,1},{1,0},{2,3},{3,2},{4,5},{5,4},{6,7},{7,6},{8,9},{9,8},{10,11... | collective-permute-start | bytes 589832 | tf_op jit(solution)/shard_map/ppermute | solution.py:443
  21.2 10.9 %collective-permute-start.3 = (f32[6,64,128]{2,1,0:T(8,128)S(1)}, f32[6,64,128]{2,1,0:T(8,128)S(1)}, u32[]{:S(2)}, u32[]{:S(2)}) collective-permute-start(f32[6,64,128]{2,1,0:T(8,128)S(1)} %get-tuple-element.18), channel_id=1, source_target_pairs={{1,2},{2,1},{3,4},{4,3},{5,6},{6,5},{7,8},{8,7},{9,10},{10,9},{11,... | collective-permute-start | bytes 589832 | tf_op jit(solution)/shard_map/ppermute | solution.py:443
  26.3 3.4 %collective-permute-start = (f32[6,8,128]{2,1,0:T(8,128)S(1)}, f32[6,8,128]{2,1,0:T(8,128)S(1)}, u32[]{:S(2)}, u32[]{:S(2)}) collective-permute-start(f32[6,8,128]{2,1,0:T(8,128)S(1)} %get-tuple-element.15), channel_id=1, source_target_pairs={{0,32},{32,0},{64,96},{96,64},{128,160},{160,128},{192,224},{224,1... | collective-permute-start | bytes 73736 | tf_op jit(solution)/shard_map/ppermute | solution.py:443
  27.3 4.8 %collective-permute-start.1 = (f32[6,8,128]{2,1,0:T(8,128)S(1)}, f32[6,8,128]{2,1,0:T(8,128)S(1)}, u32[]{:S(2)}, u32[]{:S(2)}) collective-permute-start(f32[6,8,128]{2,1,0:T(8,128)S(1)} %get-tuple-element.16), channel_id=1, source_target_pairs={{32,64},{64,32},{96,128},{128,96},{160,192},{192,160},{224,0},{0,2... | collective-permute-start | bytes 73736 | tf_op jit(solution)/shard_map/ppermute | solution.py:443
  35.0 25.7 %all-to-all-start.1 = ((f32[256,1,128]{2,1,0:T(1,128)}), f32[256,1,128]{2,1,0:T(1,128)S(1)}, u32[]{:S(2)}, u32[]{:S(2)}) async-start(f32[256,1,128]{2,1,0:T(1,128)} %bitcast.5), calls=%async_computation.1 | async-start | bytes 262144 | tf_op jit(solution)/shard_map/all_to_all | solution.py:455
  47.8 12.9 %copy-start = (s32[128]{0:T(128)S(1)}, s32[128]{0:T(128)}, u32[]{:S(2)}) copy-start(s32[128]{0:T(128)} %param.9) | copy-start | bytes 1540

commit v4 on v3

--- a/solution.py
+++ b/solution.py
@@ -81,7 +81,7 @@
     return x
 
 
-def encode_kernel(mag, vel, modes, message, parts, ends_a, ends_b, edge, slots, turned, sems, end_sems):
+def encode_kernel(mag, vel, modes, wall, message, parts, ends_a, ends_b, near, edge, slots, turned, sems, end_sems):
     count, cells = parts.shape[1], edge.shape[3]
     nmodes = 4 * count
     get_modes = pltpu.make_async_copy(modes, slots, sems.at[0])
@@ -97,6 +97,8 @@
                 pltpu.make_async_copy(ref.at[:, layer], target.at[pl.ds(3 * k, 3)], end_sems.at[k, n])
             )
             ends[-1].start()
+    ends.append(pltpu.make_async_copy(wall.at[pl.ds(0, near.shape[0])], near, sems.at[2]))
+    ends[-1].start()
     first = lax.axis_index("region") * cells
     odd_cell = (2 * (first + lanes((cells, cells))) + 1).astype(F32)
     get_modes.wait()
@@ -133,7 +135,7 @@
         copy.wait()
 
 
-def encode(mag, vel, modes):
+def encode(mag, vel, modes, wall):
     nz, nr, cells = mag.shape[1:]
     count = modes.size // 4
     layer = pltpu.VMEM((6, nr, cells), F32)
@@ -144,20 +146,21 @@
             pltpu.VMEM((4, count, 2 * cells), BF16),
             layer,
             layer,
+            pltpu.VMEM((2, *wall.shape[1:]), F32),
         ),
-        in_specs=[HBM, HBM, HBM],
-        out_specs=(VMEM,) * 4,
+        in_specs=[HBM] * 4,
+        out_specs=(VMEM,) * 5,
         scratch_shapes=[
             pltpu.VMEM((2, nz, 8, cells), F32),
             pltpu.VMEM((8, 128), jnp.int32),
             pltpu.VMEM((128, 128), F32),
-            pltpu.SemaphoreType.DMA((2,)),
+            pltpu.SemaphoreType.DMA((3,)),
             pltpu.SemaphoreType.DMA((2, 2)),
         ],
         compiler_params=params(8),
         cost_estimate=cost(3 * 2 * 1024 * 128 * 128, 1 << 20),
         name="encode",
-    )(*pinned(mag, vel, modes.reshape(8, 128)))
+    )(*pinned(mag, vel, modes.reshape(8, 128), wall))
 
 
 def wall_kernel(arrived, near, wall, *rest):
@@ -200,7 +203,7 @@
             pltpu.SemaphoreType.DMA((wall.shape[0] - near.shape[0],)),
         ],
         compiler_params=params(16),
-        cost_estimate=cost(3 * 2 * 16 * 512 * 512 * 4, 4 << 20),
+        cost_estimate=cost(1 << 10, 1 << 10),
         name="wall",
     )(arrived, *resident(near), *pinned(wall), *earlier)
 
@@ -217,58 +220,50 @@
     ]
 
 
-def pack_kernel(mag, vel, wall, ends_a, ends_b, near_wall, held, sems, wall_sem):
+def pack_kernel(mag, vel, sides, held, sems):
     nz, nr, cells = mag.shape[1:]
     lane = lanes((8, cells))
     copies = fetch(mag, vel, held, sems)
     for pair in copies:
         for copy in pair:
             copy.start()
-    get_wall = pltpu.make_async_copy(wall.at[pl.ds(0, near_wall.shape[0])], near_wall, wall_sem)
-    get_wall.start()
 
     def body(z, carry):
-        low, high = list(carry[0]), list(carry[1])
+        out = list(carry)
         for t in range(8):
-            j = z * 8 + t
-            here, wrapped = lane == j, lane == ((j + 127) & 127)
+            j = 2 * ((z & 7) * 8 + t)
+            here = (lane == j) | (lane == ((j + 127) & 127))
             for f in range(6):
                 tile = pltpu.roll(held[f // 3, f % 3, z, t * 8 : (t + 1) * 8, :], j, 1)
-                low[f] = jnp.where(here, tile, low[f])
-                high[f] = jnp.where(wrapped, tile, high[f])
-        return tuple(low), tuple(high)
-
-    zero = (jnp.zeros((8, cells), F32),) * 6
-    carry = (zero, zero)
+                out[f] = jnp.where(here, tile, out[f])
+        return tuple(out)
+
     for part, pair in enumerate(copies):
         for copy in pair:
             copy.wait()
+        if part % 2 == 0:
+            carry = (jnp.zeros((8, cells), F32),) * 6
         carry = lax.fori_loop(part * 4, part * 4 + 4, body, carry)
-    even = lax.axis_index("region") % 2 == 0
-    for f in range(6):
-        low, high = carry[0][f], carry[1][f]
-        ends_a[f] = jnp.where(even, high, low)
-        ends_b[f] = jnp.where(even, low, high)
-    get_wall.wait()
-
-
-def pack(mag, vel, wall):
+        if part % 2 == 1:
+            for f in range(6):
+                sides[f, part // 2] = carry[f]
+
+
+def pack(mag, vel):
     nz, nr, cells = mag.shape[1:]
-    edge = pltpu.VMEM((6, 8, cells), F32)
     return pl.pallas_call(
         pack_kernel,
-        out_shape=(edge, edge, pltpu.VMEM((2, *wall.shape[1:]), F32)),
-        in_specs=[HBM, HBM, HBM],
-        out_specs=(VMEM, VMEM, VMEM),
+        out_shape=pltpu.VMEM((6, 2, 8, cells), F32),
+        in_specs=[HBM, HBM],
+        out_specs=VMEM,
         scratch_shapes=[
             pltpu.VMEM((2, *mag.shape), F32),
             pltpu.SemaphoreType.DMA((2, nz // 4)),
-            pltpu.SemaphoreType.DMA,
         ],
         compiler_params=params(12),
         cost_estimate=cost(8 << 20, 4 << 20),
         name="pack",
-    )(*pinned(mag, vel, wall))
+    )(*pinned(mag, vel))
 
 
 def stencil_kernel(mag, vel, side_a, side_b, end_a, end_b, out, edge, held, stepped, factors, sides, gets, sems):
@@ -280,8 +275,12 @@
         for copy in pair:
             copy.start()
     even = lax.axis_index("region") % 2 == 0
-    sides[0] = jnp.where(even, side_b[...], side_a[...])
-    sides[1] = jnp.where(even, side_a[...], side_b[...])
+    for f in range(6):
+        for half in range(2):
+            a, b = side_a[f, half], side_b[f, half]
+            low = pltpu.roll(jnp.where(even, b, a), 1, 1)
+            high = pltpu.roll(jnp.where(even, a, b), cells - 1, 1)
+            sides[f, half] = jnp.where(lane % 2 == 0, low, high)
     even_slab = lax.axis_index("slab") % 2 == 0
     angle_step = 2.0 * math.pi / (cells * 8)
     spread = TIME_STEP * DIFFUSIVITY
@@ -300,7 +299,7 @@
 
     def layer(z, down, up):
         for t in range(nr // 8):
-            j = z * 8 + t
+            j = (z & 7) * 8 + t
             rows8 = slice(t * 8, t * 8 + 8)
             x, dr, dp, dz, sr, sp, sz = [], [], [], [], [], [], []
             for f in range(6):
@@ -314,10 +313,9 @@
                     outer = jnp.where(row == 7, here, pltpu.roll(here, 7, 0))
                 else:
                     outer = ref[c, z, t * 8 + 1 : t * 8 + 9, :]
-                far = pltpu.roll(sides[1, f], (255 - j) & 127, 1)
-                near = pltpu.roll(sides[0, f], (129 - j) & 127, 1)
-                p_next = jnp.where(lane == cells - 1, far, pltpu.roll(here, cells - 1, 1))
-                p_prev = jnp.where(lane == 0, near, pltpu.roll(here, 1, 1))
+                beyond = pltpu.roll(sides[f, z >> 3], (256 - 2 * j) & 127, 1)
+                p_next = jnp.where(lane == cells - 1, beyond, pltpu.roll(here, cells - 1, 1))
+                p_prev = jnp.where(lane == 0, beyond, pltpu.roll(here, 1, 1))
                 z_next = up(f, rows8)
                 z_prev = down(f, rows8)
                 x.append(here)
@@ -385,12 +383,12 @@
             pltpu.VMEM((2, *mag.shape), F32),
             pltpu.VMEM(mag.shape, F32),
             pltpu.VMEM((4, nr // 8, 8, cells), F32),
-            pltpu.VMEM((2, 6, 8, cells), F32),
+            pltpu.VMEM((6, 2, 8, cells), F32),
             pltpu.SemaphoreType.DMA((2, nz // 4)),
             pltpu.SemaphoreType.DMA((nz // 4,)),
         ],
         compiler_params=params(16),
-        cost_estimate=cost(40 << 20, 8 << 20),
+        cost_estimate=cost(40 << 30, 8 << 30),
         name="stencil",
     )(*pinned(mag, vel), *halos)
 
@@ -444,14 +442,14 @@
 
 
 def shards(magnetic, velocity, wall_response, mode_slots, wall_layers):
-    message, table, ends_a, ends_b = encode(magnetic, velocity, mode_slots)
+    message, table, ends_a, ends_b, near = encode(magnetic, velocity, mode_slots, wall_response)
     arrived = lax.all_to_all(message, BOTH, 0, 0, tiled=True)
     end_b = swap(ends_b, "slab", 1, False)
-    sides_a, sides_b, near = pack(magnetic, velocity, wall_response)
-    side_b = swap(sides_b, "region", 1, True)
-    side_a = swap(sides_a, "region", 0, True)
+    sides = pack(magnetic, velocity)
+    side_b = swap(sides, "region", 1, True)
+    side_a = swap(sides, "region", 0, True)
     end_a = swap(ends_a, "slab", 0, False)
-    replies = apply_wall(arrived, near, wall_response, side_a, side_b, end_a, end_b)
+    replies = apply_wall(arrived, near, wall_response, sides)
     returned = lax.all_to_all(replies, BOTH, 0, 0, tiled=True)
     stepped, edge = stencil(magnetic, velocity, side_a, side_b, end_a, end_b)
     wall_flux, magnetic_next = decode(returned, table, wall_layers, edge, stepped)

time: 62.5 us -> 58.9 us (0.942)
  starting transfers between devices: 36 us -> 32.5 us
    all_to_all x1, starting transfers between devices: 12.8 us -> 9.36 us  [shards(): returned = lax.all_to_all(replies, BOTH, 0, 0, tiled=True)]
    ppermute x4, waiting for transfers between devices: 2.39 us -> 0.01 us  [swap(): return lax.ppermute(payload, axis, pairs)]
    all_to_all x1, waiting for transfers between devices: 0.01 us -> 2.34 us  [shards(): arrived = lax.all_to_all(message, BOTH, 0, 0, tiled=True)]
  transfers between devices with their start and end apart: 6 -> 6, of which waited for: 2 -> 2; matrix products, arithmetic and copies ran while one was open for 0% -> 0% of each run, Pallas kernels for 15% -> 21%
where the time goes in v4:
time: 58.9 us; the launch traced here: 58.6 us
  starting transfers between devices  32.5 us (55%)
  Pallas kernels  16.7 us (28%)
  waiting for transfers between devices  8.68 us (15%)
  between operations  0.73 us (1%)
    all_to_all x1, starting transfers between devices, shards(): arrived = lax.all_to_all(message, BOTH, 0, 0, tiled=True)  15.7 us
    all_to_all x1, starting transfers between devices, shards(): returned = lax.all_to_all(replies, BOTH, 0, 0, tiled=True)  9.36 us
    ppermute x4, starting transfers between devices, swap(): return lax.ppermute(payload, axis, pairs)  7.49 us
    pallas_call x1, Pallas kernels, stencil(): pl.pallas_call(stencil_kernel, out_shape=(pltpu.HBM(mag.shape, F32), pltp...  6.54 us
    all_to_all x1, waiting for transfers between devices, shards(): returned = lax.all_to_all(replies, BOTH, 0, 0, tiled=True)  6.33 us
    pallas_call x1, Pallas kernels, pack(): pl.pallas_call(pack_kernel, out_shape=pltpu.VMEM((6, 2, 8, cells), F32),...  3.08 us
    pallas_call x1, Pallas kernels, apply_wall(): pl.pallas_call(wall_kernel, out_shape=jax.ShapeDtypeStruct(arrived.shape,...  2.91 us
    pallas_call x1, Pallas kernels, encode(): pl.pallas_call(encode_kernel, out_shape=(jax.ShapeDtypeStruct((count, 128...  2.62 us
  transfers between devices with their start and end apart: 6, of which 2 were waited for; matrix products, arithmetic and copies ran while one was open for 0% of the time, Pallas kernels for 21%

profile of v4, /device:TPU:1, one launch (start us, length us, event | category | flops | bytes accessed | tf_op | source)
XLA Modules:
  0.0 58.6 jit_solution(4563543845314835551)
XLA Ops:
  0.6 2.6 %encode.1 = (f32[256,128]{1,0:T(8,128)}, bf16[4,256,256]{2,1,0:T(8,128)(2,1)S(1)}, f32[6,64,128]{2,1,0:T(8,128)S(1)}, f32[6,64,128]{2,1,0:T(8,128)S(1)}, f32[2,512,512]{2,1,0:T(8,128)S(1)}) custom-call(f32[3,16,64,128]{3,2,1,0:T(8,128)} %mag.5, f32[3,16,64,128]{3,2,1,0:T(8,128)} %vel.5, s32[8,128]{1,0:T(8,128)} %bitcast.13, f32[4,512,512]{2,1,0:T(8,128)} %wall.5), custom_call_target="tpu_custom_call" | custom-call | flops 100663296 | bytes 1048576 | tf_op jit(solution)/shard_map/encode/pallas_call | solution.py:142
  3.3 15.7 %all-to-all-start = ((f32[256,1,128]{2,1,0:T(1,128)}), f32[256,1,128]{2,1,0:T(1,128)S(1)}, u32[]{:S(2)}, u32[]{:S(2)}) async-start(f32[256,1,128]{2,1,0:T(1,128)} %bitcast.2), calls=%async_computation | async-start | bytes 262144 | tf_op jit(solution)/shard_map/all_to_all | solution.py:446
  18.9 2.2 %collective-permute-start.2 = (f32[6,64,128]{2,1,0:T(8,128)S(1)}, f32[6,64,128]{2,1,0:T(8,128)S(1)}, u32[]{:S(2)}, u32[]{:S(2)}) collective-permute-start(f32[6,64,128]{2,1,0:T(8,128)S(1)} %get-tuple-element.14), channel_id=1, source_target_pairs={{0,1},{1,0},{2,3},{3,2},{4,5},{5,4},{6,7},{7,6},{8,9},{9,8},{10,11... | collective-permute-start | bytes 589832 | tf_op jit(solution)/shard_map/ppermute | solution.py:441
  21.2 1.9 %collective-permute-start.3 = (f32[6,64,128]{2,1,0:T(8,128)S(1)}, f32[6,64,128]{2,1,0:T(8,128)}, u32[]{:S(2)}, u32[]{:S(2)}) collective-permute-start(f32[6,64,128]{2,1,0:T(8,128)S(1)} %get-tuple-element.15), channel_id=1, source_target_pairs={{1,2},{2,1},{3,4},{4,3},{5,6},{6,5},{7,8},{8,7},{9,10},{10,9},{11,... | collective-permute-start | bytes 589832 | tf_op jit(solution)/shard_map/ppermute | solution.py:441
  23.1 3.1 %pack.1.rest_0_ = f32[6,2,8,128]{3,2,1,0:T(8,128)S(1)} custom-call(f32[3,16,64,128]{3,2,1,0:T(8,128)} %mag.5, f32[3,16,64,128]{3,2,1,0:T(8,128)} %vel.5), custom_call_target="tpu_custom_call" | custom-call | flops 8388608 | bytes 4194304 | tf_op jit(solution)/shard_map/pack/pallas_call | solution.py:254
  26.2 3.3 %collective-permute-start.1 = (f32[6,2,8,128]{3,2,1,0:T(8,128)S(1)}, f32[6,2,8,128]{3,2,1,0:T(8,128)S(1)}, u32[]{:S(2)}, u32[]{:S(2)}) collective-permute-start(f32[6,2,8,128]{3,2,1,0:T(8,128)S(1)} %pack.1.rest_0_), channel_id=1, source_target_pairs={{32,64},{64,32},{96,128},{128,96},{160,192},{192,160},{224,0},{0,2... | collective-permute-start | bytes 147464 | tf_op jit(solution)/shard_map/ppermute | solution.py:441
  29.5 0.0 collective-permute-start
  29.5 2.3 %all-to-all-done = f32[256,1,128]{2,1,0:T(1,128)S(1)} async-done(((f32[256,1,128]{2,1,0:T(1,128)}), f32[256,1,128]{2,1,0:T(1,128)S(1)}, u32[]{:S(2)}, u32[]{:S(2)}) %all-to-all-start) | async-done | bytes 131104 | tf_op jit(solution)/shard_map/all_to_all | solution.py:446
  31.9 2.9 %wall.4 = f32[256,128]{1,0:T(8,128)} custom-call(f32[256,128]{1,0:T(8,128)S(1)} %bitcast.10, f32[2,512,512]{2,1,0:T(8,128)S(1)} %get-tuple-element.12.near, f32[4,512,512]{2,1,0:T(8,128)} %wall.5, f32[6,2,8,128]{3,2,1,0:T(8,128)S(1)} %pack.1.rest_0_), custom_call_target="tpu_custom_call" | custom-call | flops 1024 | bytes 1024 | tf_op jit(solution)/shard_map/wall/pallas_call | solution.py:196
  34.8 9.4 %all-to-all-start.1 = ((f32[256,1,128]{2,1,0:T(1,128)}), f32[256,1,128]{2,1,0:T(1,128)S(1)}, u32[]{:S(2)}, u32[]{:S(2)}) async-start(f32[256,1,128]{2,1,0:T(1,128)} %bitcast.5), calls=%async_computation.1 | async-start | bytes 262144 | tf_op jit(solution)/shard_map/all_to_all | solution.py:453
  44.1 0.0 copy-start
  44.2 0.0 collective-permute-done.1.side_b
  44.2 0.0 collective-permute-done.side_a
  44.2 0.0 collective-permute-done.2.end_a
  44.2 0.0 collective-permute-done.3.end_b
  44.2 6.5 %stencil.1 = (f32[3,16,64,128]{3,2,1,0:T(8,128)}, f32[3,16,8,128]{3,2,1,0:T(8,128)S(1)}) custom-call(f32[3,16,64,128]{3,2,1,0:T(8,128)} %mag.5, f32[3,16,64,128]{3,2,1,0:T(8,128)} %vel.5, f32[6,2,8,128]{3,2,1,0:T(8,128)S(1)} %collective-permute-done.side_a, f32[6,2,8,128]{3,2,1,0:T(8,128)S(1)} %collective-permute-done.1.side_b, ...), custom_call_target="tpu_custom_call" | custom-call | flops 42949672960 | bytes 8589934592 | tf_op jit(solution)/shard_map/stencil/pallas_call | solution.py:377
  50.7 6.3 %all-to-all-done.1 = f32[256,1,128]{2,1,0:T(1,128)S(1)} async-done(((f32[256,1,128]{2,1,0:T(1,128)}), f32[256,1,128]{2,1,0:T(1,128)S(1)}, u32[]{:S(2)}, u32[]{:S(2)}) %all-to-all-start.1) | async-done | bytes 131104 | tf_op jit(solution)/shard_map/all_to_all | solution.py:453
  57.1 0.0 copy-done
  57.1 1.6 %decode.1 = (f32[2,16,128]{2,1,0:T(8,128)}, f32[3,16,64,128]{3,2,1,0:T(8,128)}) custom-call(f32[256,128]{1,0:T(8,128)S(1)} %bitcast.11, bf16[4,256,256]{2,1,0:T(8,128)(2,1)S(1)} %get-tuple-element.13.table, s32[1,128]{1,0:T(1,128)S(1)} %bitcast.12, f32[3,16,8,128]{3,2,1,0:T(8,128)S(1)} %get-tuple-element.16.edge, ...), custom_call_target="tpu_custom_call", output_to_operand_aliasing={{1}: (4, {})} | custom-call | flops 12582912 | bytes 1048576 | tf_op jit(solution)/shard_map/decode/pallas_call | solution.py:418
Async XLA Ops:
  3.3 28.6 %all-to-all-start = ((f32[256,1,128]{2,1,0:T(1,128)}), f32[256,1,128]{2,1,0:T(1,128)S(1)}, u32[]{:S(2)}, u32[]{:S(2)}) async-start(f32[256,1,128]{2,1,0:T(1,128)} %bitcast.2), calls=%async_computation | async-start | bytes 262144 | tf_op jit(solution)/shard_map/all_to_all | solution.py:446
  18.9 25.2 %collective-permute-start.2 = (f32[6,64,128]{2,1,0:T(8,128)S(1)}, f32[6,64,128]{2,1,0:T(8,128)S(1)}, u32[]{:S(2)}, u32[]{:S(2)}) collective-permute-start(f32[6,64,128]{2,1,0:T(8,128)S(1)} %get-tuple-element.14), channel_id=1, source_target_pairs={{0,1},{1,0},{2,3},{3,2},{4,5},{5,4},{6,7},{7,6},{8,9},{9,8},{10,11... | collective-permute-start | bytes 589832 | tf_op jit(solution)/shard_map/ppermute | solution.py:441
  21.2 23.0 %collective-permute-start.3 = (f32[6,64,128]{2,1,0:T(8,128)S(1)}, f32[6,64,128]{2,1,0:T(8,128)}, u32[]{:S(2)}, u32[]{:S(2)}) collective-permute-start(f32[6,64,128]{2,1,0:T(8,128)S(1)} %get-tuple-element.15), channel_id=1, source_target_pairs={{1,2},{2,1},{3,4},{4,3},{5,6},{6,5},{7,8},{8,7},{9,10},{10,9},{11,... | collective-permute-start | bytes 589832 | tf_op jit(solution)/shard_map/ppermute | solution.py:441
  26.2 18.0 %collective-permute-start.1 = (f32[6,2,8,128]{3,2,1,0:T(8,128)S(1)}, f32[6,2,8,128]{3,2,1,0:T(8,128)S(1)}, u32[]{:S(2)}, u32[]{:S(2)}) collective-permute-start(f32[6,2,8,128]{3,2,1,0:T(8,128)S(1)} %pack.1.rest_0_), channel_id=1, source_target_pairs={{32,64},{64,32},{96,128},{128,96},{160,192},{192,160},{224,0},{0,2... | collective-permute-start | bytes 147464 | tf_op jit(solution)/shard_map/ppermute | solution.py:441
  29.5 14.7 %collective-permute-start = (f32[6,2,8,128]{3,2,1,0:T(8,128)S(1)}, f32[6,2,8,128]{3,2,1,0:T(8,128)S(1)}, u32[]{:S(2)}, u32[]{:S(2)}) collective-permute-start(f32[6,2,8,128]{3,2,1,0:T(8,128)S(1)} %pack.1.rest_0_), channel_id=1, source_target_pairs={{0,32},{32,0},{64,96},{96,64},{128,160},{160,128},{192,224},{224,1... | collective-permute-start | bytes 147464 | tf_op jit(solution)/shard_map/ppermute | solution.py:441
  34.8 22.3 %all-to-all-start.1 = ((f32[256,1,128]{2,1,0:T(1,128)}), f32[256,1,128]{2,1,0:T(1,128)S(1)}, u32[]{:S(2)}, u32[]{:S(2)}) async-start(f32[256,1,128]{2,1,0:T(1,128)} %bitcast.5), calls=%async_computation.1 | async-start | bytes 262144 | tf_op jit(solution)/shard_map/all_to_all | solution.py:453
  44.1 12.9 %copy-start = (s32[128]{0:T(128)S(1)}, s32[128]{0:T(128)}, u32[]{:S(2)}) copy-start(s32[128]{0:T(128)} %param.9) | copy-start | bytes 1540

commit v5 on v4

--- a/solution.py
+++ b/solution.py
@@ -163,8 +163,7 @@
     )(*pinned(mag, vel, modes.reshape(8, 128), wall))
 
 
-def wall_kernel(arrived, near, wall, *rest):
-    message, held, sems = rest[-3:]
+def wall_kernel(arrived, near, wall, message, held, sems):
     count = near.shape[0]
     copies = [pltpu.make_async_copy(wall.at[count + i], held.at[i], sems.at[i]) for i in range(held.shape[0])]
     for copy in copies:
@@ -192,11 +191,11 @@
         message[r * 32 : (r + 1) * 32, :] = y
 
 
-def apply_wall(arrived, near, wall, *earlier):
+def apply_wall(arrived, near, wall):
     return pl.pallas_call(
         wall_kernel,
         out_shape=jax.ShapeDtypeStruct(arrived.shape, F32),
-        in_specs=[VMEM, VMEM, HBM] + [ANY] * len(earlier),
+        in_specs=[VMEM, VMEM, HBM],
         out_specs=VMEM,
         scratch_shapes=[
             pltpu.VMEM((wall.shape[0] - near.shape[0], *wall.shape[1:]), F32),
@@ -205,14 +204,14 @@
         compiler_params=params(16),
         cost_estimate=cost(1 << 10, 1 << 10),
         name="wall",
-    )(arrived, *resident(near), *pinned(wall), *earlier)
-
-
-def fetch(mag, vel, held, sems):
+    )(arrived, *resident(near), *pinned(wall))
+
+
+def fetch(mag, vel, first, held, sems):
     return [
         [
             pltpu.make_async_copy(
-                ref.at[:, pl.ds(part * 4, 4)], held.at[k, :, pl.ds(part * 4, 4)], sems.at[k, part]
+                ref.at[:, pl.ds(first + part * 4, 4)], held.at[k, :, pl.ds(part * 4, 4)], sems.at[k, part]
             )
             for k, ref in enumerate((mag, vel))
         ]
@@ -220,57 +219,54 @@
     ]
 
 
-def pack_kernel(mag, vel, sides, held, sems):
+def pack_kernel(mag, vel, earlier, sides, kept, held, kept_sems, held_sems):
+    del earlier
     nz, nr, cells = mag.shape[1:]
     lane = lanes((8, cells))
-    copies = fetch(mag, vel, held, sems)
-    for pair in copies:
-        for copy in pair:
-            copy.start()
-
-    def body(z, carry):
-        out = list(carry)
-        for t in range(8):
-            j = 2 * ((z & 7) * 8 + t)
-            here = (lane == j) | (lane == ((j + 127) & 127))
-            for f in range(6):
-                tile = pltpu.roll(held[f // 3, f % 3, z, t * 8 : (t + 1) * 8, :], j, 1)
-                out[f] = jnp.where(here, tile, out[f])
-        return tuple(out)
-
-    for part, pair in enumerate(copies):
-        for copy in pair:
-            copy.wait()
-        if part % 2 == 0:
-            carry = (jnp.zeros((8, cells), F32),) * 6
-        carry = lax.fori_loop(part * 4, part * 4 + 4, body, carry)
-        if part % 2 == 1:
-            for f in range(6):
-                sides[f, part // 2] = carry[f]
-
-
-def pack(mag, vel):
+    halves = ((kept, fetch(mag, vel, 0, kept, kept_sems)), (held, fetch(mag, vel, nz // 2, held, held_sems)))
+    for _, copies in halves:
+        for pair in copies:
+            for copy in pair:
+                copy.start()
+    for half, (ref, copies) in enumerate(halves):
+        out = [jnp.zeros((8, cells), F32)] * 6
+        for z in range(nz // 2):
+            if z % 4 == 0:
+                for copy in copies[z // 4]:
+                    copy.wait()
+            for t in range(8):
+                j = 2 * (z * 8 + t)
+                here = (lane == j) | (lane == ((j + 127) & 127))
+                for f in range(6):
+                    tile = pltpu.roll(ref[f // 3, f % 3, z, t * 8 : (t + 1) * 8, :], j, 1)
+                    out[f] = jnp.where(here, tile, out[f])
+        for f in range(6):
+            sides[f, half] = out[f]
+
+
+def pack(mag, vel, earlier):
     nz, nr, cells = mag.shape[1:]
     return pl.pallas_call(
         pack_kernel,
-        out_shape=pltpu.VMEM((6, 2, 8, cells), F32),
-        in_specs=[HBM, HBM],
-        out_specs=VMEM,
+        out_shape=(pltpu.VMEM((6, 2, 8, cells), F32), pltpu.VMEM((2, 3, nz // 2, nr, cells), F32)),
+        in_specs=[HBM, HBM, ANY],
+        out_specs=(VMEM, VMEM),
         scratch_shapes=[
-            pltpu.VMEM((2, *mag.shape), F32),
-            pltpu.SemaphoreType.DMA((2, nz // 4)),
+            pltpu.VMEM((2, 3, nz // 2, nr, cells), F32),
+            pltpu.SemaphoreType.DMA((2, nz // 8)),
+            pltpu.SemaphoreType.DMA((2, nz // 8)),
         ],
         compiler_params=params(12),
-        cost_estimate=cost(8 << 20, 4 << 20),
+        cost_estimate=cost(40 << 30, 8 << 30),
         name="pack",
-    )(*pinned(mag, vel))
-
-
-def stencil_kernel(mag, vel, side_a, side_b, end_a, end_b, out, edge, held, stepped, factors, sides, gets, sems):
+    )(*pinned(mag, vel), earlier)
+
+
+def stencil_kernel(mag, vel, kept, side_a, side_b, end_a, end_b, out, edge, held, stepped, factors, sides, gets, sems):
     nz, nr, cells = mag.shape[1:]
     lane = lanes((8, cells))
     row = rows((8, cells))
-    copies = fetch(mag, vel, held, gets)
+    copies = fetch(mag, vel, nz // 2, held, gets)
     for pair in copies:
         for copy in pair:
             copy.start()
@@ -298,21 +294,22 @@
         factors[3, t] = 1.0 - 2.0 * (second + (second_radial + second_axial))
 
     def layer(z, down, up):
+        field, place = whose(z)
         for t in range(nr // 8):
             j = (z & 7) * 8 + t
             rows8 = slice(t * 8, t * 8 + 8)
             x, dr, dp, dz, sr, sp, sz = [], [], [], [], [], [], []
             for f in range(6):
-                ref, c = held.at[f // 3], f % 3
-                here = ref[c, z, rows8, :]
+                ref, c = field.at[f // 3, f % 3], place
+                here = ref[c, rows8, :]
                 if t == 0:
                     inner = jnp.where(row == 0, here, pltpu.roll(here, 1, 0))
                 else:
-                    inner = ref[c, z, t * 8 - 1 : t * 8 + 7, :]
+                    inner = ref[c, t * 8 - 1 : t * 8 + 7, :]
                 if t == nr // 8 - 1:
                     outer = jnp.where(row == 7, here, pltpu.roll(here, 7, 0))
                 else:
-                    outer = ref[c, z, t * 8 + 1 : t * 8 + 9, :]
+                    outer = ref[c, t * 8 + 1 : t * 8 + 9, :]
                 beyond = pltpu.roll(sides[f, z >> 3], (256 - 2 * j) & 127, 1)
                 p_next = jnp.where(lane == cells - 1, beyond, pltpu.roll(here, cells - 1, 1))
                 p_prev = jnp.where(lane == 0, beyond, pltpu.roll(here, 1, 1))
@@ -345,52 +342,69 @@
                 edge[2, z] = jnp.where(row == 7, at_wall - by_radial * x[3], 0.0)
 
     def inside(z, step):
-        return lambda f, rows8: held[f // 3, f % 3, z + step, rows8, :]
-
-    def send(part):
-        return pltpu.make_async_copy(
-            stepped.at[:, pl.ds(part * 4, 4)], out.at[:, pl.ds(part * 4, 4)], sems.at[part]
-        )
+        field, place = whose(z, step)
+        return lambda f, rows8: field[f // 3, f % 3, place, rows8, :]
+
+    def send(n, first, count):
+        part = pl.ds(first, count)
+        return pltpu.make_async_copy(stepped.at[:, part], out.at[:, part], sems.at[n])
+
+    def whose(z, step=0):
+        if isinstance(z, int):
+            return (kept, z + step) if z + step < nz // 2 else (held, z + step - nz // 2)
+        return (kept, z + step) if in_kept[0] else (held, z + step - nz // 2)
 
     def body(z, _):
         layer(z, inside(z, -1), inside(z, 1))
         return 0
 
-    parts = nz // 4
-    for copy in copies[0]:
+    in_kept = [True]
+    sends = []
+    for n, (first, count) in enumerate(((0, 4), (4, 4), (8, 4), (12, 2), (14, 2))):
+        if first == nz // 2:
+            in_kept[0] = False
+        begin, end = first, first + count
+        if first == 0:
+            layer(0, lambda f, rows8: jnp.where(even_slab, end_b[f, rows8, :], end_a[f, rows8, :]), inside(0, 1))
+            begin = 1
+        elif first == nz // 2:
+            layer(first, inside(first, -1), inside(first, 1))
+            begin = first + 1
+        if end in (nz // 2, nz):
+            end -= 1
+        lax.fori_loop(begin, end, lambda z, n: body(z, n), 0)
+        if end == nz // 2 - 1:
+            for pair in copies:
+                for copy in pair:
+                    copy.wait()
+            layer(end, inside(end, -1), inside(end, 1))
+        if end == nz - 1:
+            layer(end, inside(end, -1), lambda f, rows8: jnp.where(even_slab, end_a[f, rows8, :], end_b[f, rows8, :]))
+        sends.append(send(n, first, count))
+        sends[-1].start()
+    for copy in sends:
         copy.wait()
-    layer(0, lambda f, rows8: jnp.where(even_slab, end_b[f, rows8, :], end_a[f, rows8, :]), inside(0, 1))
-    for part in range(parts):
-        if part < parts - 1:
-            for copy in copies[part + 1]:
-                copy.wait()
-        lax.fori_loop(max(part * 4, 1), min(part * 4 + 4, nz - 1), body, 0)
-        if part == parts - 1:
-            layer(nz - 1, inside(nz - 1, -1), lambda f, rows8: jnp.where(even_slab, end_a[f, rows8, :], end_b[f, rows8, :]))
-        send(part).start()
-    for part in range(parts):
-        send(part).wait()
-
-
-def stencil(mag, vel, *halos):
+
+
+def stencil(mag, vel, kept, *halos):
     nz, nr, cells = mag.shape[1:]
     return pl.pallas_call(
         stencil_kernel,
         out_shape=(pltpu.HBM(mag.shape, F32), pltpu.VMEM((3, nz, 8, cells), F32)),
-        in_specs=[HBM] * 2 + [VMEM] * 4,
+        in_specs=[HBM] * 2 + [VMEM] * 5,
         out_specs=(HBM, VMEM),
         scratch_shapes=[
-            pltpu.VMEM((2, *mag.shape), F32),
+            pltpu.VMEM(kept.shape, F32),
             pltpu.VMEM(mag.shape, F32),
             pltpu.VMEM((4, nr // 8, 8, cells), F32),
             pltpu.VMEM((6, 2, 8, cells), F32),
-            pltpu.SemaphoreType.DMA((2, nz // 4)),
-            pltpu.SemaphoreType.DMA((nz // 4,)),
+            pltpu.SemaphoreType.DMA((2, nz // 8)),
+            pltpu.SemaphoreType.DMA((5,)),
         ],
         compiler_params=params(16),
-        cost_estimate=cost(40 << 30, 8 << 30),
+        cost_estimate=cost(40 << 20, 8 << 20),
         name="stencil",
-    )(*pinned(mag, vel), *halos)
+    )(*pinned(mag, vel), *resident(kept), *halos)
 
 
 def decode_kernel(arrived, table, layers, edge, held, flux, out, fixed, sem):
@@ -445,13 +459,13 @@
     message, table, ends_a, ends_b, near = encode(magnetic, velocity, mode_slots, wall_response)
     arrived = lax.all_to_all(message, BOTH, 0, 0, tiled=True)
     end_b = swap(ends_b, "slab", 1, False)
-    sides = pack(magnetic, velocity)
+    end_a = swap(ends_a, "slab", 0, False)
+    replies = apply_wall(arrived, near, wall_response)
+    returned = lax.all_to_all(replies, BOTH, 0, 0, tiled=True)
+    sides, kept = pack(magnetic, velocity, replies)
     side_b = swap(sides, "region", 1, True)
     side_a = swap(sides, "region", 0, True)
-    end_a = swap(ends_a, "slab", 0, False)
-    replies = apply_wall(arrived, near, wall_response, sides)
-    returned = lax.all_to_all(replies, BOTH, 0, 0, tiled=True)
-    stepped, edge = stencil(magnetic, velocity, side_a, side_b, end_a, end_b)
+    stepped, edge = stencil(magnetic, velocity, kept, side_a, side_b, end_a, end_b)
     wall_flux, magnetic_next = decode(returned, table, wall_layers, edge, stepped)
     return magnetic_next, wall_flux
 

time: 58.9 us -> 56.2 us (0.954)
  waiting for transfers between devices: 8.68 us -> 12 us
  starting transfers between devices: 32.5 us -> 29.3 us
  Pallas kernels: 16.7 us -> 13.9 us
    all_to_all x1, waiting for transfers between devices: 2.34 us -> 8.72 us  [shards(): arrived = lax.all_to_all(message, BOTH, 0, 0, tiled=True)]
    all_to_all x1, waiting for transfers between devices: 6.33 us -> 0.01 us  [shards(): returned = lax.all_to_all(replies, BOTH, 0, 0, tiled=True)]
    all_to_all x1, starting transfers between devices: 9.36 us -> 5.44 us  [shards(): returned = lax.all_to_all(replies, BOTH, 0, 0, tiled=True)]
    ppermute x4, waiting for transfers between devices: 0.01 us -> 3.23 us  [swap(): return lax.ppermute(payload, axis, pairs)]
    pallas_call x1, Pallas kernels: 6.54 us -> 4.27 us  [stencil(): pl.pallas_call(stencil_kernel, out_shape=(pltpu.HBM(mag.shape, F32), pltp...]
    ppermute x4, starting transfers between devices: 7.49 us -> 8.19 us  [swap(): return lax.ppermute(payload, axis, pairs)]
  transfers between devices with their start and end apart: 6 -> 6, of which waited for: 2 -> 3; matrix products, arithmetic and copies ran while one was open for 0% -> 0% of each run, Pallas kernels for 21% -> 17%
where the time goes in v5:
time: 56.2 us; the launch traced here: 55.9 us
  starting transfers between devices  29.3 us (52%)
  Pallas kernels  13.9 us (25%)
  waiting for transfers between devices  12 us (21%)
  between operations  0.71 us (1%)
    all_to_all x1, starting transfers between devices, shards(): arrived = lax.all_to_all(message, BOTH, 0, 0, tiled=True)  15.7 us
    all_to_all x1, waiting for transfers between devices, shards(): arrived = lax.all_to_all(message, BOTH, 0, 0, tiled=True)  8.72 us
    ppermute x4, starting transfers between devices, swap(): return lax.ppermute(payload, axis, pairs)  8.19 us
    all_to_all x1, starting transfers between devices, shards(): returned = lax.all_to_all(replies, BOTH, 0, 0, tiled=True)  5.44 us
    pallas_call x1, Pallas kernels, stencil(): pl.pallas_call(stencil_kernel, out_shape=(pltpu.HBM(mag.shape, F32), pltp...  4.27 us
    ppermute x4, waiting for transfers between devices, swap(): return lax.ppermute(payload, axis, pairs)  3.23 us
    pallas_call x1, Pallas kernels, apply_wall(): pl.pallas_call(wall_kernel, out_shape=jax.ShapeDtypeStruct(arrived.shape,...  2.91 us
    pallas_call x1, Pallas kernels, encode(): pl.pallas_call(encode_kernel, out_shape=(jax.ShapeDtypeStruct((count, 128...  2.62 us
  transfers between devices with their start and end apart: 6, of which 3 were waited for; matrix products, arithmetic and copies ran while one was open for 0% of the time, Pallas kernels for 17%

profile of v5, /device:TPU:1, one launch (start us, length us, event | category | flops | bytes accessed | tf_op | source)
XLA Modules:
  0.0 55.9 jit_solution(13231168452288870937)
XLA Ops:
  0.6 2.6 %encode.1 = (f32[256,128]{1,0:T(8,128)}, bf16[4,256,256]{2,1,0:T(8,128)(2,1)S(1)}, f32[6,64,128]{2,1,0:T(8,128)S(1)}, f32[6,64,128]{2,1,0:T(8,128)S(1)}, f32[2,512,512]{2,1,0:T(8,128)S(1)}) custom-call(f32[3,16,64,128]{3,2,1,0:T(8,128)} %mag.5, f32[3,16,64,128]{3,2,1,0:T(8,128)} %vel.5, s32[8,128]{1,0:T(8,128)} %bitcast.13, f32[4,512,512]{2,1,0:T(8,128)} %wall.5), custom_call_target="tpu_custom_call" | custom-call | flops 100663296 | bytes 1048576 | tf_op jit(solution)/shard_map/encode/pallas_call | solution.py:142
  3.3 15.7 %all-to-all-start = ((f32[256,1,128]{2,1,0:T(1,128)}), f32[256,1,128]{2,1,0:T(1,128)S(1)}, u32[]{:S(2)}, u32[]{:S(2)}) async-start(f32[256,1,128]{2,1,0:T(1,128)} %bitcast.2), calls=%async_computation | async-start | bytes 262144 | tf_op jit(solution)/shard_map/all_to_all | solution.py:460
  18.9 2.2 %collective-permute-start.2 = (f32[6,64,128]{2,1,0:T(8,128)S(1)}, f32[6,64,128]{2,1,0:T(8,128)S(1)}, u32[]{:S(2)}, u32[]{:S(2)}) collective-permute-start(f32[6,64,128]{2,1,0:T(8,128)S(1)} %get-tuple-element.18), channel_id=1, source_target_pairs={{0,1},{1,0},{2,3},{3,2},{4,5},{5,4},{6,7},{7,6},{8,9},{9,8},{10,11... | collective-permute-start | bytes 589832 | tf_op jit(solution)/shard_map/ppermute | solution.py:455
  21.2 1.9 %collective-permute-start.3 = (f32[6,64,128]{2,1,0:T(8,128)S(1)}, f32[6,64,128]{2,1,0:T(8,128)S(1)}, u32[]{:S(2)}, u32[]{:S(2)}) collective-permute-start(f32[6,64,128]{2,1,0:T(8,128)S(1)} %get-tuple-element.19), channel_id=1, source_target_pairs={{1,2},{2,1},{3,4},{4,3},{5,6},{6,5},{7,8},{8,7},{9,10},{10,9},{11,... | collective-permute-start | bytes 589832 | tf_op jit(solution)/shard_map/ppermute | solution.py:455
  23.1 8.7 %all-to-all-done = f32[256,1,128]{2,1,0:T(1,128)S(1)} async-done(((f32[256,1,128]{2,1,0:T(1,128)}), f32[256,1,128]{2,1,0:T(1,128)S(1)}, u32[]{:S(2)}, u32[]{:S(2)}) %all-to-all-start) | async-done | bytes 131104 | tf_op jit(solution)/shard_map/all_to_all | solution.py:460
  31.8 2.9 %wall.4.earlier = f32[256,128]{1,0:T(8,128)} custom-call(f32[256,128]{1,0:T(8,128)S(1)} %bitcast.10, f32[2,512,512]{2,1,0:T(8,128)S(1)} %get-tuple-element.14.near, f32[4,512,512]{2,1,0:T(8,128)} %wall.5), custom_call_target="tpu_custom_call" | custom-call | flops 1024 | bytes 1024 | tf_op jit(solution)/shard_map/wall/pallas_call | solution.py:195
  34.7 5.4 %all-to-all-start.1 = ((f32[256,1,128]{2,1,0:T(1,128)}), f32[256,1,128]{2,1,0:T(1,128)S(1)}, u32[]{:S(2)}, u32[]{:S(2)}) async-start(f32[256,1,128]{2,1,0:T(1,128)} %bitcast.5), calls=%async_computation.1 | async-start | bytes 262144 | tf_op jit(solution)/shard_map/all_to_all | solution.py:464
  40.2 2.6 %pack.1 = (f32[6,2,8,128]{3,2,1,0:T(8,128)S(1)}, f32[2,3,8,64,128]{4,3,2,1,0:T(8,128)S(1)}) custom-call(f32[3,16,64,128]{3,2,1,0:T(8,128)} %mag.5, f32[3,16,64,128]{3,2,1,0:T(8,128)} %vel.5, f32[256,128]{1,0:T(8,128)} %wall.4.earlier), custom_call_target="tpu_custom_call" | custom-call | flops 42949672960 | bytes 8589934592 | tf_op jit(solution)/shard_map/pack/pallas_call | solution.py:249
  42.8 4.0 %collective-permute-start.1 = (f32[6,2,8,128]{3,2,1,0:T(8,128)S(1)}, f32[6,2,8,128]{3,2,1,0:T(8,128)S(1)}, u32[]{:S(2)}, u32[]{:S(2)}) collective-permute-start(f32[6,2,8,128]{3,2,1,0:T(8,128)S(1)} %get-tuple-element.17), channel_id=1, source_target_pairs={{32,64},{64,32},{96,128},{128,96},{160,192},{192,160},{224,0},{0,2... | collective-permute-start | bytes 147464 | tf_op jit(solution)/shard_map/ppermute | solution.py:455
  46.8 0.0 collective-permute-start
  46.8 0.0 collective-permute-done.2.end_a
  46.8 0.0 collective-permute-done.3.end_b
  46.8 1.8 %collective-permute-done.1.side_b = f32[6,2,8,128]{3,2,1,0:T(8,128)S(1)} collective-permute-done((f32[6,2,8,128]{3,2,1,0:T(8,128)S(1)}, f32[6,2,8,128]{3,2,1,0:T(8,128)S(1)}, u32[]{:S(2)}, u32[]{:S(2)}) %collective-permute-start.1) | collective-permute-done | bytes 49184 | tf_op jit(solution)/shard_map/ppermute | solution.py:455
  48.7 1.4 %collective-permute-done.side_a = f32[6,2,8,128]{3,2,1,0:T(8,128)S(1)} collective-permute-done((f32[6,2,8,128]{3,2,1,0:T(8,128)S(1)}, f32[6,2,8,128]{3,2,1,0:T(8,128)S(1)}, u32[]{:S(2)}, u32[]{:S(2)}) %collective-permute-start) | collective-permute-done | bytes 49184 | tf_op jit(solution)/shard_map/ppermute | solution.py:455
  50.0 0.0 copy-start
  50.0 4.3 %stencil.1 = (f32[3,16,64,128]{3,2,1,0:T(8,128)}, f32[3,16,8,128]{3,2,1,0:T(8,128)S(1)}) custom-call(f32[3,16,64,128]{3,2,1,0:T(8,128)} %mag.5, f32[3,16,64,128]{3,2,1,0:T(8,128)} %vel.5, f32[2,3,8,64,128]{4,3,2,1,0:T(8,128)S(1)} %get-tuple-element.16.kept, f32[6,2,8,128]{3,2,1,0:T(8,128)S(1)} %collective-permute-done.side_a, ...), custom_call_target="tpu_custom_call" | custom-call | flops 41943040 | bytes 8388608 | tf_op jit(solution)/shard_map/stencil/pallas_call | solution.py:391
  54.3 0.0 all-to-all-done.1
  54.3 0.0 copy-done
  54.3 1.6 %decode.1 = (f32[2,16,128]{2,1,0:T(8,128)}, f32[3,16,64,128]{3,2,1,0:T(8,128)}) custom-call(f32[256,128]{1,0:T(8,128)S(1)} %bitcast.11, bf16[4,256,256]{2,1,0:T(8,128)(2,1)S(1)} %get-tuple-element.15.table, s32[1,128]{1,0:T(1,128)S(1)} %bitcast.12, f32[3,16,8,128]{3,2,1,0:T(8,128)S(1)} %get-tuple-element.20.edge, ...), custom_call_target="tpu_custom_call", output_to_operand_aliasing={{1}: (4, {})} | custom-call | flops 12582912 | bytes 1048576 | tf_op jit(solution)/shard_map/decode/pallas_call | solution.py:432
Async XLA Ops:
  3.3 28.5 %all-to-all-start = ((f32[256,1,128]{2,1,0:T(1,128)}), f32[256,1,128]{2,1,0:T(1,128)S(1)}, u32[]{:S(2)}, u32[]{:S(2)}) async-start(f32[256,1,128]{2,1,0:T(1,128)} %bitcast.2), calls=%async_computation | async-start | bytes 262144 | tf_op jit(solution)/shard_map/all_to_all | solution.py:460
  18.9 27.9 %collective-permute-start.2 = (f32[6,64,128]{2,1,0:T(8,128)S(1)}, f32[6,64,128]{2,1,0:T(8,128)S(1)}, u32[]{:S(2)}, u32[]{:S(2)}) collective-permute-start(f32[6,64,128]{2,1,0:T(8,128)S(1)} %get-tuple-element.18), channel_id=1, source_target_pairs={{0,1},{1,0},{2,3},{3,2},{4,5},{5,4},{6,7},{7,6},{8,9},{9,8},{10,11... | collective-permute-start | bytes 589832 | tf_op jit(solution)/shard_map/ppermute | solution.py:455
  21.2 25.7 %collective-permute-start.3 = (f32[6,64,128]{2,1,0:T(8,128)S(1)}, f32[6,64,128]{2,1,0:T(8,128)S(1)}, u32[]{:S(2)}, u32[]{:S(2)}) collective-permute-start(f32[6,64,128]{2,1,0:T(8,128)S(1)} %get-tuple-element.19), channel_id=1, source_target_pairs={{1,2},{2,1},{3,4},{4,3},{5,6},{6,5},{7,8},{8,7},{9,10},{10,9},{11,... | collective-permute-start | bytes 589832 | tf_op jit(solution)/shard_map/ppermute | solution.py:455
  34.7 19.6 %all-to-all-start.1 = ((f32[256,1,128]{2,1,0:T(1,128)}), f32[256,1,128]{2,1,0:T(1,128)S(1)}, u32[]{:S(2)}, u32[]{:S(2)}) async-start(f32[256,1,128]{2,1,0:T(1,128)} %bitcast.5), calls=%async_computation.1 | async-start | bytes 262144 | tf_op jit(solution)/shard_map/all_to_all | solution.py:464
  42.8 5.9 %collective-permute-start.1 = (f32[6,2,8,128]{3,2,1,0:T(8,128)S(1)}, f32[6,2,8,128]{3,2,1,0:T(8,128)S(1)}, u32[]{:S(2)}, u32[]{:S(2)}) collective-permute-start(f32[6,2,8,128]{3,2,1,0:T(8,128)S(1)} %get-tuple-element.17), channel_id=1, source_target_pairs={{32,64},{64,32},{96,128},{128,96},{160,192},{192,160},{224,0},{0,2... | collective-permute-start | bytes 147464 | tf_op jit(solution)/shard_map/ppermute | solution.py:455
  46.8 3.2 %collective-permute-start = (f32[6,2,8,128]{3,2,1,0:T(8,128)S(1)}, f32[6,2,8,128]{3,2,1,0:T(8,128)S(1)}, u32[]{:S(2)}, u32[]{:S(2)}) collective-permute-start(f32[6,2,8,128]{3,2,1,0:T(8,128)S(1)} %get-tuple-element.17), channel_id=1, source_target_pairs={{0,32},{32,0},{64,96},{96,64},{128,160},{160,128},{192,224},{224,1... | collective-permute-start | bytes 147464 | tf_op jit(solution)/shard_map/ppermute | solution.py:455
  50.0 4.3 %copy-start = (s32[128]{0:T(128)S(1)}, s32[128]{0:T(128)}, u32[]{:S(2)}) copy-start(s32[128]{0:T(128)} %param.9) | copy-start | bytes 1540

commit v6 on v5

--- a/solution.py
+++ b/solution.py
@@ -81,7 +81,7 @@
     return x
 
 
-def encode_kernel(mag, vel, modes, wall, message, parts, ends_a, ends_b, near, edge, slots, turned, sems, end_sems):
+def encode_kernel(mag, vel, modes, wall, message, parts, ends_a, ends_b, near, rows_out, edge, slots, turned, sems, end_sems):
     count, cells = parts.shape[1], edge.shape[3]
     nmodes = 4 * count
     get_modes = pltpu.make_async_copy(modes, slots, sems.at[0])
@@ -130,7 +130,9 @@
         both = dot(parts[i], weights, NT)
         both = (both[:, 0:128] + both[:, 128:256]) * jnp.concatenate(scale, 0)
         out = jnp.where(lane == i, both, out)
-    message[...] = out
+    rows_out[...] = out
+    ends.append(pltpu.make_async_copy(rows_out, message, sems.at[3]))
+    ends[-1].start()
     for copy in ends:
         copy.wait()
 
@@ -142,19 +144,20 @@
     return pl.pallas_call(
         encode_kernel,
         out_shape=(
-            jax.ShapeDtypeStruct((count, 128), F32),
+            pltpu.HBM((count, 128), F32),
             pltpu.VMEM((4, count, 2 * cells), BF16),
             layer,
             layer,
             pltpu.VMEM((2, *wall.shape[1:]), F32),
         ),
         in_specs=[HBM] * 4,
-        out_specs=(VMEM,) * 5,
+        out_specs=(HBM,) + (VMEM,) * 4,
         scratch_shapes=[
+            pltpu.VMEM((count, 128), F32),
             pltpu.VMEM((2, nz, 8, cells), F32),
             pltpu.VMEM((8, 128), jnp.int32),
             pltpu.VMEM((128, 128), F32),
-            pltpu.SemaphoreType.DMA((3,)),
+            pltpu.SemaphoreType.DMA((4,)),
             pltpu.SemaphoreType.DMA((2, 2)),
         ],
         compiler_params=params(8),
@@ -407,7 +410,7 @@
     )(*pinned(mag, vel), *resident(kept), *halos)
 
 
-def decode_kernel(arrived, table, layers, edge, held, flux, out, fixed, sem):
+def decode_kernel(arrived, table, layers, edge, held, flux, out, fixed, total_out, sems):
     del held
     nz, cells = flux.shape[1:]
     high, low = split(jnp.transpose(arrived[...], (1, 0)))
@@ -418,12 +421,15 @@
         total = total + dot(pair, table[i], NN)
     total = total[:, 0:cells] + total[:, cells : 2 * cells]
     total = (total[0 : 2 * nz] + total[2 * nz : 4 * nz]).reshape(2, nz, cells)
+    total_out[...] = total
+    put_flux = pltpu.make_async_copy(total_out, flux, sems.at[0])
+    put_flux.start()
     thickness = layers[...].astype(F32) * (1.0 / LW)
     for c in range(2):
         fixed[c] = edge[c] - (thickness * total[c])[:, None, :] * edge[2]
-    put = pltpu.make_async_copy(fixed, out.at[1:3, :, 56:64, :], sem)
+    put = pltpu.make_async_copy(fixed, out.at[1:3, :, 56:64, :], sems.at[1])
     put.start()
-    flux[...] = total
+    put_flux.wait()
     put.wait()
 
 
@@ -432,12 +438,16 @@
     return pl.pallas_call(
         decode_kernel,
         out_shape=(
-            jax.ShapeDtypeStruct((2, nz, cells), F32),
+            pltpu.HBM((2, nz, cells), F32),
             pltpu.HBM(held.shape, F32),
         ),
         in_specs=[VMEM, VMEM, VMEM, VMEM, HBM],
-        out_specs=(VMEM, HBM),
-        scratch_shapes=[pltpu.VMEM((2, nz, 8, cells), F32), pltpu.SemaphoreType.DMA],
+        out_specs=(HBM, HBM),
+        scratch_shapes=[
+            pltpu.VMEM((2, nz, 8, cells), F32),
+            pltpu.VMEM((2, nz, cells), F32),
+            pltpu.SemaphoreType.DMA((2,)),
+        ],
         input_output_aliases={4: 1},
         compiler_params=params(8),
         cost_estimate=cost(12 << 20, 1 << 20),

time: 56.2 us -> 55.6 us (0.989)
    pallas_call x2, Pallas kernels: 4.18 us -> 3.6 us  [the longest x1 2.63 us: encode(): pl.pallas_call(encode_kernel, out_shape=(pltpu.HBM((count, 128), F32), pl...]
  transfers between devices with their start and end apart: 6 -> 6, of which waited for: 3 -> 3; matrix products, arithmetic and copies ran while one was open for 0% -> 0% of each run, Pallas kernels for 17% -> 18%
where the time goes in v6:
time: 55.6 us; the launch traced here: 55.3 us
  starting transfers between devices  29.3 us (53%)
  Pallas kernels  13.4 us (24%)
  waiting for transfers between devices  12 us (22%)
  between operations  0.71 us (1%)
    all_to_all x1, starting transfers between devices, shards(): arrived = lax.all_to_all(message, BOTH, 0, 0, tiled=True)  15.7 us
    all_to_all x1, waiting for transfers between devices, shards(): arrived = lax.all_to_all(message, BOTH, 0, 0, tiled=True)  8.72 us
    ppermute x4, starting transfers between devices, swap(): return lax.ppermute(payload, axis, pairs)  8.19 us
    all_to_all x1, starting transfers between devices, shards(): returned = lax.all_to_all(replies, BOTH, 0, 0, tiled=True)  5.44 us
    pallas_call x1, Pallas kernels, stencil(): pl.pallas_call(stencil_kernel, out_shape=(pltpu.HBM(mag.shape, F32), pltp...  4.27 us
    ppermute x4, waiting for transfers between devices, swap(): return lax.ppermute(payload, axis, pairs)  3.23 us
    pallas_call x1, Pallas kernels, apply_wall(): pl.pallas_call(wall_kernel, out_shape=jax.ShapeDtypeStruct(arrived.shape,...  2.91 us
    pallas_call x1, Pallas kernels, encode(): pl.pallas_call(encode_kernel, out_shape=(pltpu.HBM((count, 128), F32), pl...  2.63 us
  transfers between devices with their start and end apart: 6, of which 3 were waited for; matrix products, arithmetic and copies ran while one was open for 0% of the time, Pallas kernels for 18%

profile of v6, /device:TPU:1, one launch (start us, length us, event | category | flops | bytes accessed | tf_op | source)
XLA Modules:
  0.0 55.3 jit_solution(10636225247768386396)
XLA Ops:
  0.6 2.6 %encode.1 = (f32[256,128]{1,0:T(8,128)}, bf16[4,256,256]{2,1,0:T(8,128)(2,1)S(1)}, f32[6,64,128]{2,1,0:T(8,128)S(1)}, f32[6,64,128]{2,1,0:T(8,128)S(1)}, f32[2,512,512]{2,1,0:T(8,128)S(1)}) custom-call(f32[3,16,64,128]{3,2,1,0:T(8,128)} %mag.5, f32[3,16,64,128]{3,2,1,0:T(8,128)} %vel.5, s32[8,128]{1,0:T(8,128)} %bitcast.14, f32[4,512,512]{2,1,0:T(8,128)} %wall.5), custom_call_target="tpu_custom_call" | custom-call | flops 100663296 | bytes 1048576 | tf_op jit(solution)/shard_map/encode/pallas_call | solution.py:144
  3.3 15.7 %all-to-all-start = ((f32[256,1,128]{2,1,0:T(1,128)}), f32[256,1,128]{2,1,0:T(1,128)S(1)}, u32[]{:S(2)}, u32[]{:S(2)}) async-start(f32[256,1,128]{2,1,0:T(1,128)} %bitcast.13), calls=%async_computation | async-start | bytes 262144 | tf_op jit(solution)/shard_map/all_to_all | solution.py:470
  18.9 2.2 %collective-permute-start.2 = (f32[6,64,128]{2,1,0:T(8,128)S(1)}, f32[6,64,128]{2,1,0:T(8,128)S(1)}, u32[]{:S(2)}, u32[]{:S(2)}) collective-permute-start(f32[6,64,128]{2,1,0:T(8,128)S(1)} %get-tuple-element.18), channel_id=1, source_target_pairs={{0,1},{1,0},{2,3},{3,2},{4,5},{5,4},{6,7},{7,6},{8,9},{9,8},{10,11... | collective-permute-start | bytes 589832 | tf_op jit(solution)/shard_map/ppermute | solution.py:465
  21.2 1.9 %collective-permute-start.3 = (f32[6,64,128]{2,1,0:T(8,128)S(1)}, f32[6,64,128]{2,1,0:T(8,128)S(1)}, u32[]{:S(2)}, u32[]{:S(2)}) collective-permute-start(f32[6,64,128]{2,1,0:T(8,128)S(1)} %get-tuple-element.19), channel_id=1, source_target_pairs={{1,2},{2,1},{3,4},{4,3},{5,6},{6,5},{7,8},{8,7},{9,10},{10,9},{11,... | collective-permute-start | bytes 589832 | tf_op jit(solution)/shard_map/ppermute | solution.py:465
  23.1 8.7 %all-to-all-done = f32[256,1,128]{2,1,0:T(1,128)S(1)} async-done(((f32[256,1,128]{2,1,0:T(1,128)}), f32[256,1,128]{2,1,0:T(1,128)S(1)}, u32[]{:S(2)}, u32[]{:S(2)}) %all-to-all-start) | async-done | bytes 131104 | tf_op jit(solution)/shard_map/all_to_all | solution.py:470
  31.8 2.9 %wall.4.earlier = f32[256,128]{1,0:T(8,128)} custom-call(f32[256,128]{1,0:T(8,128)S(1)} %bitcast.10, f32[2,512,512]{2,1,0:T(8,128)S(1)} %get-tuple-element.14.near, f32[4,512,512]{2,1,0:T(8,128)} %wall.5), custom_call_target="tpu_custom_call" | custom-call | flops 1024 | bytes 1024 | tf_op jit(solution)/shard_map/wall/pallas_call | solution.py:198
  34.7 5.4 %all-to-all-start.1 = ((f32[256,1,128]{2,1,0:T(1,128)}), f32[256,1,128]{2,1,0:T(1,128)S(1)}, u32[]{:S(2)}, u32[]{:S(2)}) async-start(f32[256,1,128]{2,1,0:T(1,128)} %bitcast.5), calls=%async_computation.1 | async-start | bytes 262144 | tf_op jit(solution)/shard_map/all_to_all | solution.py:474
  40.2 2.6 %pack.1 = (f32[6,2,8,128]{3,2,1,0:T(8,128)S(1)}, f32[2,3,8,64,128]{4,3,2,1,0:T(8,128)S(1)}) custom-call(f32[3,16,64,128]{3,2,1,0:T(8,128)} %mag.5, f32[3,16,64,128]{3,2,1,0:T(8,128)} %vel.5, f32[256,128]{1,0:T(8,128)} %wall.4.earlier), custom_call_target="tpu_custom_call" | custom-call | flops 42949672960 | bytes 8589934592 | tf_op jit(solution)/shard_map/pack/pallas_call | solution.py:252
  42.8 4.0 %collective-permute-start.1 = (f32[6,2,8,128]{3,2,1,0:T(8,128)S(1)}, f32[6,2,8,128]{3,2,1,0:T(8,128)S(1)}, u32[]{:S(2)}, u32[]{:S(2)}) collective-permute-start(f32[6,2,8,128]{3,2,1,0:T(8,128)S(1)} %get-tuple-element.17), channel_id=1, source_target_pairs={{32,64},{64,32},{96,128},{128,96},{160,192},{192,160},{224,0},{0,2... | collective-permute-start | bytes 147464 | tf_op jit(solution)/shard_map/ppermute | solution.py:465
  46.8 0.0 collective-permute-start
  46.8 0.0 collective-permute-done.2.end_a
  46.8 0.0 collective-permute-done.3.end_b
  46.8 1.8 %collective-permute-done.1.side_b = f32[6,2,8,128]{3,2,1,0:T(8,128)S(1)} collective-permute-done((f32[6,2,8,128]{3,2,1,0:T(8,128)S(1)}, f32[6,2,8,128]{3,2,1,0:T(8,128)S(1)}, u32[]{:S(2)}, u32[]{:S(2)}) %collective-permute-start.1) | collective-permute-done | bytes 49184 | tf_op jit(solution)/shard_map/ppermute | solution.py:465
  48.7 1.4 %collective-permute-done.side_a = f32[6,2,8,128]{3,2,1,0:T(8,128)S(1)} collective-permute-done((f32[6,2,8,128]{3,2,1,0:T(8,128)S(1)}, f32[6,2,8,128]{3,2,1,0:T(8,128)S(1)}, u32[]{:S(2)}, u32[]{:S(2)}) %collective-permute-start) | collective-permute-done | bytes 49184 | tf_op jit(solution)/shard_map/ppermute | solution.py:465
  50.1 0.0 copy-start
  50.1 4.3 %stencil.1 = (f32[3,16,64,128]{3,2,1,0:T(8,128)}, f32[3,16,8,128]{3,2,1,0:T(8,128)S(1)}) custom-call(f32[3,16,64,128]{3,2,1,0:T(8,128)} %mag.5, f32[3,16,64,128]{3,2,1,0:T(8,128)} %vel.5, f32[2,3,8,64,128]{4,3,2,1,0:T(8,128)S(1)} %get-tuple-element.16.kept, f32[6,2,8,128]{3,2,1,0:T(8,128)S(1)} %collective-permute-done.side_a, ...), custom_call_target="tpu_custom_call" | custom-call | flops 41943040 | bytes 8388608 | tf_op jit(solution)/shard_map/stencil/pallas_call | solution.py:394
  54.3 0.0 all-to-all-done.1
  54.3 0.0 copy-done
  54.4 1.0 %decode.1 = (f32[2,16,128]{2,1,0:T(8,128)}, f32[3,16,64,128]{3,2,1,0:T(8,128)}) custom-call(f32[256,128]{1,0:T(8,128)S(1)} %bitcast.11, bf16[4,256,256]{2,1,0:T(8,128)(2,1)S(1)} %get-tuple-element.15.table, s32[1,128]{1,0:T(1,128)S(1)} %bitcast.12, f32[3,16,8,128]{3,2,1,0:T(8,128)S(1)} %get-tuple-element.20.edge, ...), custom_call_target="tpu_custom_call", output_to_operand_aliasing={{1}: (4, {})} | custom-call | flops 12582912 | bytes 1048576 | tf_op jit(solution)/shard_map/decode/pallas_call | solution.py:438
Async XLA Ops:
  3.3 28.5 %all-to-all-start = ((f32[256,1,128]{2,1,0:T(1,128)}), f32[256,1,128]{2,1,0:T(1,128)S(1)}, u32[]{:S(2)}, u32[]{:S(2)}) async-start(f32[256,1,128]{2,1,0:T(1,128)} %bitcast.13), calls=%async_computation | async-start | bytes 262144 | tf_op jit(solution)/shard_map/all_to_all | solution.py:470
  18.9 27.9 %collective-permute-start.2 = (f32[6,64,128]{2,1,0:T(8,128)S(1)}, f32[6,64,128]{2,1,0:T(8,128)S(1)}, u32[]{:S(2)}, u32[]{:S(2)}) collective-permute-start(f32[6,64,128]{2,1,0:T(8,128)S(1)} %get-tuple-element.18), channel_id=1, source_target_pairs={{0,1},{1,0},{2,3},{3,2},{4,5},{5,4},{6,7},{7,6},{8,9},{9,8},{10,11... | collective-permute-start | bytes 589832 | tf_op jit(solution)/shard_map/ppermute | solution.py:465
  21.2 25.7 %collective-permute-start.3 = (f32[6,64,128]{2,1,0:T(8,128)S(1)}, f32[6,64,128]{2,1,0:T(8,128)S(1)}, u32[]{:S(2)}, u32[]{:S(2)}) collective-permute-start(f32[6,64,128]{2,1,0:T(8,128)S(1)} %get-tuple-element.19), channel_id=1, source_target_pairs={{1,2},{2,1},{3,4},{4,3},{5,6},{6,5},{7,8},{8,7},{9,10},{10,9},{11,... | collective-permute-start | bytes 589832 | tf_op jit(solution)/shard_map/ppermute | solution.py:465
  34.7 19.6 %all-to-all-start.1 = ((f32[256,1,128]{2,1,0:T(1,128)}), f32[256,1,128]{2,1,0:T(1,128)S(1)}, u32[]{:S(2)}, u32[]{:S(2)}) async-start(f32[256,1,128]{2,1,0:T(1,128)} %bitcast.5), calls=%async_computation.1 | async-start | bytes 262144 | tf_op jit(solution)/shard_map/all_to_all | solution.py:474
  42.8 5.9 %collective-permute-start.1 = (f32[6,2,8,128]{3,2,1,0:T(8,128)S(1)}, f32[6,2,8,128]{3,2,1,0:T(8,128)S(1)}, u32[]{:S(2)}, u32[]{:S(2)}) collective-permute-start(f32[6,2,8,128]{3,2,1,0:T(8,128)S(1)} %get-tuple-element.17), channel_id=1, source_target_pairs={{32,64},{64,32},{96,128},{128,96},{160,192},{192,160},{224,0},{0,2... | collective-permute-start | bytes 147464 | tf_op jit(solution)/shard_map/ppermute | solution.py:465
  46.8 3.2 %collective-permute-start = (f32[6,2,8,128]{3,2,1,0:T(8,128)S(1)}, f32[6,2,8,128]{3,2,1,0:T(8,128)S(1)}, u32[]{:S(2)}, u32[]{:S(2)}) collective-permute-start(f32[6,2,8,128]{3,2,1,0:T(8,128)S(1)} %get-tuple-element.17), channel_id=1, source_target_pairs={{0,32},{32,0},{64,96},{96,64},{128,160},{160,128},{192,224},{224,1... | collective-permute-start | bytes 147464 | tf_op jit(solution)/shard_map/ppermute | solution.py:465
  50.1 4.3 %copy-start = (s32[128]{0:T(128)S(1)}, s32[128]{0:T(128)}, u32[]{:S(2)}) copy-start(s32[128]{0:T(128)} %param.9) | copy-start | bytes 1540
